TPU v7x, 32 devices: a whole 2x2x4 slice. The times are simulated.
32 devices in a mesh: dom: 16 (over z, y, x), feat: 2 (over core).
Axes of the slice: x: 2, y: 2, z: 4, core: 2. Of those that a mesh axis runs over, the one named last changes fastest.
Arguments:
- features: bfloat16 [65536, 256], P('dom', 'feat'), may hold values from -6 to 6
- self_weight: bfloat16 [256, 256], P('feat'), may hold values from -0.375 to 0.375
- neighbor_weight: bfloat16 [256, 256], P('feat'), may hold values from -0.375 to 0.375
- tile_values: bfloat16 [2560, 128, 128], P('dom'), may hold values from 0 to 1
- tile_row: int32 [2560], P('dom'), may hold values from 0 to 31
- tile_owner: int32 [2560], P('dom'), may hold values from 0 to 15
- send_tile: int32 [256], P('dom'), may hold values from 0 to 31
- tile_count: int32 [16], P('dom'), may hold values from 26 to 160, as said below
- hub_panel: bfloat16 [65536, 32], P('dom'), may hold values from 0 to 1
- hub_rows: int32 [32], P('dom'), may hold values from 0 to 4095
- cotangent: bfloat16 [65536, 256], P('dom', 'feat'), may hold values from -6 to 6
Outputs:
- layer_out: bfloat16 [65536, 256], P('dom', 'feat')
- self_grad: float32 [256, 256], P('feat')
- neighbor_grad: float32 [256, 256], P('feat')
- input_grad: float32 [65536, 256], P('dom', 'feat')
Inputs may be any that keep to these rules, and one draw needn't show every extreme that they name: `tile_count`: one partition has exactly 160 live slots in every draw.
All inputs are finite; a program needn't handle non-finite values.
Results may differ from a plain program's by a relative error of at most 0.011.
The roundings to bfloat16 on the way count: a program that leaves them out, or rounds other values in their place, can miss the bound.
Values may be sent and summed in bfloat16 or wider, within the bound.
A program may use at most 128 MiB of HBM per device.

v0:
```python
import math

import jax
import jax.numpy as jnp
from jax import lax
from jax.sharding import PartitionSpec as P


def shards(
    features,
    self_weight,
    neighbor_weight,
    tile_values,
    tile_row,
    tile_owner,
    send_tile,
    tile_count,
    hub_panel,
    hub_rows,
    cotangent,
):
    rows_dev, half_width = features.shape
    tile_cap, tile_edge = (tile_values.shape[0], tile_values.shape[1])
    tiles_dev = rows_dev // tile_edge
    dom_size = lax.axis_size("dom")
    local_tiles = features.reshape(tiles_dev, tile_edge, half_width)
    outgoing = local_tiles[send_tile]
    hub_local = features[hub_rows]
    incoming = lax.all_to_all(outgoing, "dom", split_axis=0, concat_axis=0, tiled=True)
    hub_feats = lax.all_gather(hub_local, "dom", axis=0, tiled=True)
    live_mask = (jnp.arange(tile_cap) < tile_count[0]).astype(jnp.float32)
    columns = incoming[tile_owner]
    products = (
        jnp.einsum("kij,kjf->kif", tile_values, columns, preferred_element_type=jnp.float32)
        * live_mask[:, None, None]
    )
    neighbor_sums = jax.ops.segment_sum(products, tile_row, num_segments=tiles_dev).reshape(
        rows_dev, half_width
    )
    neighbor_sums = neighbor_sums + jnp.dot(
        hub_panel, hub_feats, preferred_element_type=jnp.float32
    )
    wide_values = tile_values.astype(jnp.float32)
    tile_squares = jnp.sum(wide_values * wide_values, axis=2) * live_mask[:, None]
    squares = jax.ops.segment_sum(tile_squares, tile_row, num_segments=tiles_dev).reshape(rows_dev)
    wide_panel = hub_panel.astype(jnp.float32)
    squares = squares + jnp.sum(wide_panel * wide_panel, axis=1)
    inverse_norm = lax.rsqrt(1.0 + squares)
    aggregate = (neighbor_sums * inverse_norm[:, None]).astype(jnp.bfloat16)
    partial_sums = jnp.dot(features, self_weight, preferred_element_type=jnp.float32) + jnp.dot(
        aggregate, neighbor_weight, preferred_element_type=jnp.float32
    )
    preact = lax.psum_scatter(partial_sums, "feat", scatter_dimension=1, tiled=True)
    layer_out = jnp.maximum(preact, 0.0).astype(jnp.bfloat16)
    slopes = jnp.where(preact > 0, cotangent.astype(jnp.float32), 0.0).astype(jnp.bfloat16)
    slopes_full = lax.all_gather(slopes, "feat", axis=1, tiled=True)
    self_term = jnp.einsum("vi,vo->io", features, slopes_full, preferred_element_type=jnp.float32)
    neighbor_term = jnp.einsum(
        "vi,vo->io", aggregate, slopes_full, preferred_element_type=jnp.float32
    )
    self_sum, neighbor_sum = lax.psum((self_term, neighbor_term), "dom")
    factor = 1.0 / math.sqrt(rows_dev * dom_size)
    direct = jnp.einsum("vo,io->vi", slopes_full, self_weight, preferred_element_type=jnp.float32)
    agg_slopes = (
        jnp.einsum("vo,io->vi", slopes_full, neighbor_weight, preferred_element_type=jnp.float32)
        * inverse_norm[:, None]
    ).astype(jnp.bfloat16)
    slope_tiles = agg_slopes.reshape(tiles_dev, tile_edge, half_width)[tile_row]
    tile_back = (
        jnp.einsum("kji,kjf->kif", tile_values, slope_tiles, preferred_element_type=jnp.float32)
        * live_mask[:, None, None]
    )
    owner_terms = jax.ops.segment_sum(tile_back, tile_owner, num_segments=dom_size).astype(
        jnp.bfloat16
    )
    hub_term = jnp.einsum("vh,vf->hf", hub_panel, agg_slopes, preferred_element_type=jnp.float32)
    returned = lax.all_to_all(owner_terms, "dom", split_axis=0, concat_axis=0, tiled=True)
    hub_grad = lax.psum_scatter(hub_term, "dom", scatter_dimension=0, tiled=True)
    owner_back = jax.ops.segment_sum(
        returned.astype(jnp.float32), send_tile, num_segments=tiles_dev
    ).reshape(rows_dev, half_width)
    input_grad = (direct + owner_back).at[hub_rows].add(hub_grad)
    return (layer_out, self_sum * factor, neighbor_sum * factor, input_grad)


def solution(mesh):
    placed = (
        P("dom", "feat"),
        P("feat", None),
        P("feat", None),
        P("dom", None, None),
        P("dom"),
        P("dom"),
        P("dom"),
        P("dom"),
        P("dom", None),
        P("dom"),
        P("dom", "feat"),
    )
    return jax.shard_map(
        shards,
        mesh=mesh,
        in_specs=placed,
        out_specs=(P("dom", "feat"), P("feat", None), P("feat", None), P("dom", "feat")),
        check_vma=False,
    )
```

profile of v0, /device:TPU:0, one launch (start us, length us, event | category | flops | bytes accessed | tf_op | source)
XLA Modules:
  0.0 360.2 jit_solution(7276717252366761268)
XLA Ops:
  8.4 1.4 gather_fusion
  9.8 8.3 %all-to-all-start = ((bf16[16,128,128]{2,1,0:T(8,128)(2,1)}), bf16[16,128,128]{2,1,0:T(8,128)(2,1)S(1)}, u32[]{:S(2)}, u32[]{:S(2)}) async-start(bf16[16,128,128]{2,1,0:T(8,128)(2,1)} %gather_fusion), calls=%async_computation | async-start | bytes 1048576 | tf_op jit(solution)/shard_map/all_to_all | solution.py:29
  18.9 5.3 %multiply_reduce_fusion = f32[160,128]{1,0:T(8,128)S(1)} fusion(bf16[160,128,128]{2,1,0:T(8,128)(2,1)} %param.14), kind=kLoop, calls=%fused_computation.10 | loop fusion | flops 7843840 | bytes 5324800 | tf_op jit(solution)/shard_map/reduce_sum | solution.py:44
  25.4 42.5 %all-gather.1 = bf16[16,2,128]{2,1,0:T(2,128)(2,1)} all-gather(bf16[1,2,128]{2,1,0:T(2,128)(2,1)S(1)} %bitcast.56), channel_id=2, replica_groups=mesh['dom'=16,'feat'=2] {'dom'}, dimensions={0}, use_global_device_ids=true | all-gather | bytes 8704 | tf_op jit(solution)/shard_map/all_gather | solution.py:30
  67.9 1.4 scatter_custom_fusion.1
  69.4 2.7 fusion.12
  72.1 7.6 %gather_fusion.1 = bf16[160,128,128]{2,1,0:T(8,128)(2,1)} fusion(bf16[16,128,128]{2,1,0:T(8,128)(2,1)S(1)} %all-to-all-done, s32[1024]{0:T(1024)S(1)} %pad_clamp_fusion.2), kind=kCustom, calls=%fused_computation.1 | custom fusion | bytes 10486400 | tf_op jit(solution)/shard_map/gather | solution.py:32
  79.7 11.9 %multiply_bitcast_fusion.1 = f32[160,128,128]{1,2,0:T(8,128)} fusion(f32[160]{0:T(256)S(1)} %compare_convert_fusion, bf16[160,128,128]{2,1,0:T(8,128)(2,1)} %gather_fusion.1, bf16[160,128,128]{2,1,0:T(8,128)(2,1)} %param.14), kind=kOutput, calls=%fused_computation.11 | convolution fusion | flops 673710080 | bytes 20972160 | tf_op jit(solution)/shard_map/kij,kjf->kif/dot_general | solution.py:34
  91.6 11.7 %copy.33 = f32[160,128,128]{2,1,0:T(8,128)} copy(f32[160,128,128]{1,2,0:T(8,128)} %multiply_bitcast_fusion.1) | data formatting | bytes 20971520 | tf_op jit(solution)/shard_map/mul | solution.py:34
  103.6 21.2 %scatter_fusion = f32[32,128,128]{2,1,0:T(8,128)S(1)} fusion(f32[32,128,128]{2,1,0:T(8,128)S(1)} %broadcast.38.clone, s32[160]{0:T(256)S(1)} %copy-done.10, f32[160,128,128]{2,1,0:T(8,128)} %copy.33), kind=kCustom, calls=%fused_computation.4 | custom fusion | flops 2621440 | bytes 31457920 | tf_op jit(solution)/shard_map/scatter-add | solution.py:37
  124.8 1.8 copy.46
  126.6 2.1 fusion.2
  129.8 4.9 %convolution_add_fusion = f32[4096,256]{1,0:T(8,128)} fusion(f32[4096,256]{1,0:T(8,128)} %fusion.12, bf16[4096,128]{0,1:T(8,128)(2,1)S(1)} %fusion.2, bf16[128,256]{1,0:T(8,128)(2,1)S(1)} %copy-done.6), kind=kOutput, calls=%fused_computation.12 | convolution fusion | flops 269484032 | bytes 9502720 | tf_op jit(solution)/shard_map/dot_general | solution.py:50
  135.0 7.8 %reduce-scatter.2.cloned.1.call-done = f32[4096,128]{1,0:T(8,128)} async-done(((f32[4096,256]{1,0:T(8,128)}), f32[4096,128]{1,0:T(8,128)}) %reduce-scatter.2.cloned.1.call-update) | async-done | bytes 2097168 | tf_op jit(solution)/shard_map/reduce_scatter | solution.py:53
  142.8 3.3 select_convert_fusion
  150.4 7.5 %all-gather.4.cloned.1.call-done = bf16[4096,256]{1,0:T(8,128)(2,1)} async-done(((bf16[4096,128]{1,0:T(8,128)(2,1)}), bf16[4096,256]{1,0:T(8,128)(2,1)}) %all-gather.4.cloned.1.call-update) | async-done | bytes 2097168 | tf_op jit(solution)/shard_map/all_gather | solution.py:56
  157.9 2.4 fusion.3
  161.0 8.0 %gather_fusion.3 = bf16[160,128,128]{2,1,0:T(8,128)(2,1)} fusion(bf16[32,128,128]{2,1,0:T(8,128)(2,1)S(1)} %bitcast.53, s32[1024]{0:T(1024)} %pad_clamp_fusion), kind=kCustom, calls=%fused_computation.3 | custom fusion | bytes 10486400 | tf_op jit(solution)/shard_map/gather | solution.py:68
  169.1 10.5 %multiply_bitcast_fusion = f32[160,128,128]{1,2,0:T(8,128)} fusion(f32[160]{0:T(256)S(1)} %copy-done.9, bf16[160,128,128]{2,1,0:T(8,128)(2,1)} %gather_fusion.3, bf16[160,128,128]{2,1,0:T(8,128)(2,1)} %param.14), kind=kOutput, calls=%fused_computation.9 | convolution fusion | flops 673710080 | bytes 20972160 | tf_op jit(solution)/shard_map/kji,kjf->kif/dot_general | solution.py:70
  179.6 11.8 %copy.39 = f32[160,128,128]{2,1,0:T(8,128)} copy(f32[160,128,128]{1,2,0:T(8,128)} %multiply_bitcast_fusion) | data formatting | bytes 20971520 | tf_op jit(solution)/shard_map/mul | solution.py:70
  191.4 21.2 %scatter_fusion.1 = f32[16,128,128]{2,1,0:T(8,128)S(1)} fusion(f32[16,128,128]{2,1,0:T(8,128)S(1)} %broadcast_in_dim.42, s32[160]{0:T(256)S(1)} %copy-done.12, f32[160,128,128]{2,1,0:T(8,128)} %copy.39), kind=kCustom, calls=%fused_computation.6 | custom fusion | flops 2621440 | bytes 31457920 | tf_op jit(solution)/shard_map/scatter-add | solution.py:73
  213.6 7.0 %all-to-all-start.1 = ((bf16[16,128,128]{2,1,0:T(8,128)(2,1)}), bf16[16,128,128]{2,1,0:T(8,128)(2,1)}, u32[]{:S(2)}, u32[]{:S(2)}) async-start(bf16[16,128,128]{2,1,0:T(8,128)(2,1)} %convert_element_type.46), calls=%async_computation.2 | async-start | bytes 1048576 | tf_op jit(solution)/shard_map/all_to_all | solution.py:77
  220.6 3.5 fusion.13
  224.1 1.4 convolution_bitcast_fusion.1
  225.6 1.7 convolution_bitcast_fusion.2
  227.2 77.2 %all-reduce = f32[32,128]{1,0:T(8,128)S(1)} all-reduce(f32[32,128]{1,0:T(8,128)S(1)} %convolution_bitcast_fusion.2), channel_id=4, replica_groups=mesh['dom'=16,'feat'=2] {'dom'}, use_global_device_ids=true, to_apply=%region_9.10.clone | all-reduce | flops 4096 | bytes 32768
  304.5 32.1 %all-reduce.4.cloned.1.call-done = (f32[128,256]{0,1:T(8,128)}, f32[128,256]{0,1:T(8,128)}) async-done(((f32[128,256]{0,1:T(8,128)}, f32[128,256]{0,1:T(8,128)}), (f32[128,256]{0,1:T(8,128)}, f32[128,256]{0,1:T(8,128)})) %all-reduce.4.cloned.1.call-update) | async-done | bytes 262160 | tf_op jit(solution)/shard_map/psum | solution.py:61
  339.1 2.1 convert_element_type.47
  341.2 1.6 broadcast.38
  342.8 3.7 %scatter_fusion.2 = f32[32,128,128]{2,1,0:T(8,128)} fusion(f32[32,128,128]{2,1,0:T(8,128)} %broadcast.38, s32[16]{0:T(128)S(1)} %copy-done.14, f32[16,128,128]{2,1,0:T(8,128)} %convert_element_type.47), kind=kCustom, calls=%fused_computation.7 | custom fusion | flops 262144 | bytes 3145792 | tf_op jit(solution)/shard_map/scatter-add | solution.py:79
  346.5 3.6 %convolution_add_fusion.1 = f32[4096,128]{1,0:T(8,128)} fusion(f32[4096,128]{1,0:T(8,128)} %bitcast.54, bf16[4096,256]{1,0:T(8,128)(2,1)S(1)} %copy-done.1, bf16[128,256]{1,0:T(8,128)(2,1)S(1)} %copy-done.7), kind=kOutput, calls=%fused_computation.14 | convolution fusion | flops 268959744 | bytes 6356992 | tf_op jit(solution)/shard_map/vo,io->vi/dot_general | solution.py:63
  350.1 3.6 scatter_custom_fusion.4
  (61 shorter events, 12.0 us)
Async XLA Ops:
  7.2 1.2 copy-start
  9.8 62.3 %all-to-all-start = ((bf16[16,128,128]{2,1,0:T(8,128)(2,1)}), bf16[16,128,128]{2,1,0:T(8,128)(2,1)S(1)}, u32[]{:S(2)}, u32[]{:S(2)}) async-start(bf16[16,128,128]{2,1,0:T(8,128)(2,1)} %gather_fusion), calls=%async_computation | async-start | bytes 1048576 | tf_op jit(solution)/shard_map/all_to_all | solution.py:29
  18.1 124.7 %reduce-scatter.2.cloned.1.call-start = ((), (), s32[]{:S(2)}) async-start(), calls=%async_computation.3 | async-start | bytes 6291456 | tf_op jit(solution)/shard_map/reduce_scatter | solution.py:53
  18.8 60.9 %copy-start.8 = (f32[160]{0:T(256)}, f32[160]{0:T(256)S(1)}, u32[]{:S(2)}) copy-start(f32[160]{0:T(256)S(1)} %compare_convert_fusion) | copy-start | bytes 1924
  18.9 5.4 %copy-start.15 = (s32[2]{0:T(128)S(1)}, s32[2]{0:T(128)}, u32[]{:S(2)}) copy-start(s32[2]{0:T(128)} %param.20) | copy-start | bytes 28
  18.9 49.0 %copy-start.10 = (s32[160]{0:T(256)S(1)}, s32[160]{0:T(256)}, u32[]{:S(2)}) copy-start(s32[160]{0:T(256)} %param.15) | copy-start | bytes 1924
  18.9 50.4 %copy-start.11 = (s32[160]{0:T(256)S(1)}, s32[160]{0:T(256)}, u32[]{:S(2)}) copy-start(s32[160]{0:T(256)} %param.16) | copy-start | bytes 1924
  18.9 50.4 %copy-start.5 = (bf16[4096,32]{0,1:T(8,128)(2,1)S(1)}, bf16[4096,32]{0,1:T(8,128)(2,1)}, u32[]{:S(2)}) copy-start(bf16[4096,32]{0,1:T(8,128)(2,1)} %param.19) | copy-start | bytes 786436
  18.9 50.5 %copy-start.7 = (bf16[128,256]{1,0:T(8,128)(2,1)S(1)}, bf16[128,256]{1,0:T(8,128)(2,1)}, u32[]{:S(2)}) copy-start(bf16[128,256]{1,0:T(8,128)(2,1)} %param.12) | copy-start | bytes 196612
  24.2 0.6 copy-start.13
  126.6 3.2 copy-start.6
  128.7 1.1 copy-start.3
  134.7 23.2 %all-gather.4.cloned.1.call-start = ((), (), s32[]{:S(2)}) async-start(), calls=%async_computation.4 | async-start | bytes 3145728 | tf_op jit(solution)/shard_map/all_gather | solution.py:56
  142.8 6.5 %copy-start.4 = (f32[4096,128]{1,0:T(8,128)S(1)}, f32[4096,128]{1,0:T(8,128)}, u32[]{:S(2)}) copy-start(f32[4096,128]{1,0:T(8,128)} %reduce-scatter.2.cloned.1.call-done) | copy-start | bytes 6291460
  160.3 8.7 %copy-start.2 = (bf16[4096,128]{0,1:T(8,128)(2,1)}, bf16[4096,128]{0,1:T(8,128)(2,1)S(1)}, u32[]{:S(2)}) copy-start(bf16[4096,128]{0,1:T(8,128)(2,1)S(1)} %fusion.3) | copy-start | bytes 3145732
  161.0 8.0 %copy-start.9 = (f32[160]{0:T(256)S(1)}, f32[160]{0:T(256)}, u32[]{:S(2)}) copy-start(f32[160]{0:T(256)} %copy-done.8) | copy-start | bytes 1924
  179.6 11.9 %copy-start.12 = (s32[160]{0:T(256)S(1)}, s32[160]{0:T(256)}, u32[]{:S(2)}) copy-start(s32[160]{0:T(256)} %param.16) | copy-start | bytes 1924
  213.6 10.6 %copy-start.1 = (bf16[4096,256]{1,0:T(8,128)(2,1)S(1)}, bf16[4096,256]{1,0:T(8,128)(2,1)}, u32[]{:S(2)}) copy-start(bf16[4096,256]{1,0:T(8,128)(2,1)} %all-gather.4.cloned.1.call-done) | copy-start | bytes 6291460
  213.6 125.5 %all-to-all-start.1 = ((bf16[16,128,128]{2,1,0:T(8,128)(2,1)}), bf16[16,128,128]{2,1,0:T(8,128)(2,1)}, u32[]{:S(2)}, u32[]{:S(2)}) async-start(bf16[16,128,128]{2,1,0:T(8,128)(2,1)} %convert_element_type.46), calls=%async_computation.2 | async-start | bytes 1048576 | tf_op jit(solution)/shard_map/all_to_all | solution.py:77
  220.6 116.0 %all-reduce.4.cloned.1.call-start = ((), (), s32[]{:S(2)}) async-start(), calls=%async_computation.5 | async-start | bytes 524288 | tf_op jit(solution)/shard_map/psum | solution.py:61
  337.5 5.2 %copy-start.14 = (s32[16]{0:T(128)S(1)}, s32[16]{0:T(128)}, u32[]{:S(2)}) copy-start(s32[16]{0:T(128)} %param.17) | copy-start | bytes 196
Sparse Core Ops, SparseCore 0:
  134.9 7.9 reduce-scatter.1
  146.3 11.6 all-gather.3
  228.1 108.4 all-reduce.3
where the time goes:
time: 362 us; the launch traced here: 360 us
  blocking collectives  120 us (33%)
  other arithmetic  66.9 us (18%)
  local copies, waits for them, and re-layouts  50.4 us (14%)
  waiting for transfers between devices  47.5 us (13%)
  matrix products  44.7 us (12%)
  starting transfers between devices  15.7 us (4%)
  between operations  15.3 us (4%)
    unnamed x1, blocking collectives  77.2 us
    all_gather x1, blocking collectives, shards(): hub_feats = lax.all_gather(hub_local, 'dom', axis=0, tiled=True)  42.5 us
    psum x1, waiting for transfers between devices, shards(): self_sum, neighbor_sum = lax.psum((self_term, neighbor_term), 'dom')  32.1 us
    scatter-add x1, other arithmetic, shards(): jax.ops.segment_sum(tile_back, tile_owner, num_segments=dom_size)  21.2 us
    scatter-add x1, other arithmetic, shards(): jax.ops.segment_sum(products, tile_row, num_segments=tiles_dev)  21.2 us
    dot_general x1, matrix products, shards(): jnp.einsum('kij,kjf->kif', tile_values, columns, preferred_element_type=j...  11.9 us
    mul x1, local copies, waits for them, and re-layouts, shards(): jnp.einsum('kji,kjf->kif', tile_values, slope_tiles, preferred_element_ty...  11.8 us
    mul x1, local copies, waits for them, and re-layouts, shards(): jnp.einsum('kij,kjf->kif', tile_values, columns, preferred_element_type=j...  11.7 us
  transfers between devices with their start and end apart: 5, of which 3 were waited for; matrix products, arithmetic and copies ran while one was open for 6% of the time, Pallas kernels for 0%

commit v1 on v0

v1 whole, which is shorter than its diff:
```python
import functools
import math

import jax
import jax.numpy as jnp
from jax import lax
from jax.experimental import pallas as pl
from jax.experimental.pallas import tpu as pltpu
from jax.sharding import PartitionSpec as P

F32 = jnp.float32
BF16 = jnp.bfloat16
VMEM_BYTES = 58 * 2**20
UNROLL = 4


def vmem():
    return pl.BlockSpec(memory_space=pltpu.VMEM)


def smem():
    return pl.BlockSpec(memory_space=pltpu.SMEM)


def dot(a, b, dims=((1,), (0,))):
    return lax.dot_general(a, b, (dims, ((), ())), preferred_element_type=F32)


def greet(n, me, feat, with_sibling):
    barrier = pltpu.get_barrier_semaphore()

    def hello(d, carry):
        pl.semaphore_signal(
            barrier, inc=1, device_id={"dom": lax.rem(me + d, n)}, device_id_type=pl.DeviceIdType.MESH
        )
        return carry

    lax.fori_loop(1, n, hello, 0)
    if with_sibling:
        pl.semaphore_signal(barrier, inc=1, device_id={"feat": 1 - feat}, device_id_type=pl.DeviceIdType.MESH)
    pl.semaphore_wait(barrier, n if with_sibling else n - 1)


def exchange_kernel(
    n, hub_dev, feat_ref, cot_ref, ws_ref, wn_ref, send_ref, hub_ref,
    cols_ref, x_ref, c_ref, wso_ref, wno_ref,
    stage, send_sem, recv_sem, fsend_sem, frecv_sem, loc_sem, esend_sem, erecv_sem,
):
    me = lax.axis_index("dom")
    feat = lax.axis_index("feat")
    edge = feat_ref.shape[1]
    rows = edge * feat_ref.shape[0]
    pad = stage.shape[1] - edge
    half = feat_ref.shape[2]
    greet(n, me, feat, True)

    row_ids = lax.broadcasted_iota(jnp.int32, (edge, half), 0)
    out_ids = lax.broadcasted_iota(jnp.int32, (pad, half), 0)
    hub_block = jnp.zeros((pad, half), F32)
    for h in range(hub_dev):
        r = hub_ref[h]
        tile = feat_ref[r // edge].astype(F32)
        row = jnp.sum(jnp.where(row_ids == r % edge, tile, 0.0), axis=0, keepdims=True)
        hub_block = jnp.where(out_ids == h, row, hub_block)
    hub_block = hub_block.astype(BF16)

    def peer_copy(d):
        return pltpu.make_async_remote_copy(
            src_ref=stage.at[d], dst_ref=cols_ref.at[me, :, 0:half],
            send_sem=send_sem.at[d], recv_sem=recv_sem.at[d],
            device_id={"dom": lax.rem(me + d, n)}, device_id_type=pl.DeviceIdType.MESH,
        )

    def forward(q):
        return pltpu.make_async_remote_copy(
            src_ref=cols_ref.at[q, :, 0:half], dst_ref=cols_ref.at[q, :, half:2 * half],
            send_sem=fsend_sem.at[q], recv_sem=frecv_sem.at[q],
            device_id={"feat": 1 - feat}, device_id_type=pl.DeviceIdType.MESH,
        )

    def send(d, carry):
        q = lax.rem(me + d, n)
        stage[d, 0:edge, :] = feat_ref[send_ref[q]]
        stage[d, edge:, :] = hub_block
        peer_copy(d).start()
        return carry

    lax.fori_loop(1, n, send, 0)
    cols_ref[me, 0:edge, 0:half] = feat_ref[send_ref[me]]
    cols_ref[me, edge:, 0:half] = hub_block
    forward(me).start()

    extras = [
        pltpu.make_async_remote_copy(
            src_ref=src, dst_ref=dst, send_sem=esend_sem.at[i], recv_sem=erecv_sem.at[i],
            device_id={"feat": 1 - feat}, device_id_type=pl.DeviceIdType.MESH,
        )
        for i, (src, dst) in enumerate((
            (feat_ref, x_ref.at[:, :, half:2 * half]),
            (cot_ref, c_ref.at[:, :, half:2 * half]),
            (ws_ref, wso_ref),
            (wn_ref, wno_ref),
        ))
    ]
    for copy in extras:
        copy.start()
    locals_ = [
        pltpu.make_async_copy(feat_ref, x_ref.at[:, :, 0:half], loc_sem.at[0]),
        pltpu.make_async_copy(cot_ref, c_ref.at[:, :, 0:half], loc_sem.at[1]),
    ]
    for copy in locals_:
        copy.start()

    def arrive(d, carry):
        peer_copy(d).wait_recv()
        forward(lax.rem(me - d + n, n)).start()
        return carry

    lax.fori_loop(1, n, arrive, 0)
    for copy in locals_:
        copy.wait()
    for copy in extras:
        copy.wait()

    def finish(d, carry):
        peer_copy(d).wait_send()
        return carry

    lax.fori_loop(1, n, finish, 0)

    def finish_forward(q, carry):
        forward(q).wait()
        return carry

    lax.fori_loop(0, n, finish_forward, 0)


def slot_loop(count, step):
    full = count // UNROLL

    def many(i, carry):
        for u in range(UNROLL):
            step(i * UNROLL + u)
        return carry

    lax.fori_loop(0, full, many, 0)

    def single(k, carry):
        step(k)
        return carry

    lax.fori_loop(full * UNROLL, count, single, 0)


def local_kernel(
    hub_dev, feat_ref, row_ref, owner_ref, count_ref,
    cols_ref, x_ref, c_ref, ws_ref, wn_ref, wso_ref, wno_ref, val_ref, panel_ref,
    out_ref, grad_ref, direct_ref, terms_ref,
    acc, sq, slopes_t, terms_t, hub_s,
):
    f = feat_ref[0]
    tiles, edge, wide = x_ref.shape
    half = wide // 2
    n = cols_ref.shape[0]
    hubs = panel_ref.shape[2]
    pad = cols_ref.shape[1] - edge
    count = count_ref[0]

    def local_order(w):
        return jnp.where(f == 0, w, jnp.concatenate([w[:, half:], w[:, :half]], axis=1))

    ws_own = local_order(ws_ref[...].astype(F32)).astype(BF16)
    wn_own = local_order(wn_ref[...].astype(F32)).astype(BF16)
    ws_all = jnp.concatenate([ws_own, local_order(wso_ref[...].astype(F32)).astype(BF16)], axis=0)
    wn_all = jnp.concatenate([wn_own, local_order(wno_ref[...].astype(F32)).astype(BF16)], axis=0)

    hub_ids = lax.broadcasted_iota(jnp.int32, (hubs, n * pad), 0)
    place = lax.broadcasted_iota(jnp.int32, (hubs, n * pad), 1)
    pick = (hub_ids // hub_dev == place // pad) & (hub_ids % hub_dev == place % pad)
    hub_rows = cols_ref[:, edge:, :].reshape(n * pad, wide)
    hub_feats = dot(jnp.where(pick, 1.0, 0.0).astype(BF16), hub_rows).astype(BF16)

    def start(t, carry):
        panel = panel_ref[t]
        acc[t] = dot(panel, hub_feats)
        sq[t] = jnp.zeros((edge, edge), F32)
        return carry

    lax.fori_loop(0, tiles, start, 0)

    def ahead(k):
        values = val_ref[k]
        row = row_ref[k]
        acc[row] += dot(values, cols_ref[owner_ref[k], 0:edge, :])
        wide_values = values.astype(F32)
        sq[row] += wide_values * wide_values

    slot_loop(count, ahead)

    grad_ref[...] = jnp.zeros_like(grad_ref)
    hub_s[...] = jnp.zeros_like(hub_s)

    def dense(t, carry):
        panel = panel_ref[t]
        wide_panel = panel.astype(F32)
        squares = jnp.sum(sq[t], axis=1, keepdims=True) + jnp.sum(wide_panel * wide_panel, axis=1, keepdims=True)
        inverse = lax.rsqrt(1.0 + squares)
        aggregate = (acc[t] * inverse).astype(BF16)
        x = x_ref[t]
        preact = dot(x, ws_all) + dot(aggregate, wn_all)
        out_ref[t] = jnp.maximum(preact[:, :half], 0.0).astype(BF16)
        slopes = jnp.where(preact > 0, c_ref[t].astype(F32), 0.0).astype(BF16)
        direct_ref[t] = dot(slopes, ws_own, ((1,), (1,)))
        back = dot(slopes, wn_own, ((1,), (1,))) * inverse
        back_t = back.T.astype(BF16)
        slopes_t[t] = back_t
        hub_s[...] += dot(back_t, panel)
        left = jnp.concatenate([x[:, :half], aggregate[:, :half]], axis=1)
        grad_ref[...] += dot(left, slopes, ((0,), (0,)))
        return carry

    lax.fori_loop(0, tiles, dense, 0)

    def clear(o, carry):
        terms_t[o] = jnp.zeros((half, edge), F32)
        return carry

    lax.fori_loop(0, n, clear, 0)

    def behind(k):
        terms_t[owner_ref[k]] += dot(slopes_t[row_ref[k]], val_ref[k])

    slot_loop(count, behind)

    hub_terms = hub_s[...].T
    high = hub_terms.astype(BF16)
    low = (hub_terms - high.astype(F32)).astype(BF16)
    ids = lax.broadcasted_iota(jnp.int32, (n * pad, hubs), 1)
    spot = lax.broadcasted_iota(jnp.int32, (n * pad, hubs), 0)
    same = ids // hub_dev == spot // pad
    put_high = jnp.where(same & (spot % pad == ids % hub_dev), 1.0, 0.0).astype(BF16)
    put_low = jnp.where(same & (spot % pad == ids % hub_dev + hub_dev), 1.0, 0.0).astype(BF16)
    blocks = dot(put_high, high) + dot(put_low, low)
    terms_ref[:, edge:, :] = blocks.reshape(n, pad, half).astype(BF16)

    def emit(o, carry):
        terms_ref[o, 0:edge, :] = terms_t[o].T.astype(BF16)
        return carry

    lax.fori_loop(0, n, emit, 0)


def return_kernel(n, reduce_here, factor, *refs):
    if reduce_here:
        (terms_ref, grad_ref, back_ref, self_ref, neigh_ref,
         send_sem, recv_sem, gstage, gin, gall, rsend, rrecv, asend, arecv) = refs
    else:
        terms_ref, back_ref, send_sem, recv_sem = refs
    me = lax.axis_index("dom")
    feat = lax.axis_index("feat")
    greet(n, me, feat, False)

    def copy_to(d, src, dst, ssem, rsem):
        return pltpu.make_async_remote_copy(
            src_ref=src, dst_ref=dst, send_sem=ssem.at[d], recv_sem=rsem.at[d],
            device_id={"dom": lax.rem(me + d, n)}, device_id_type=pl.DeviceIdType.MESH,
        )

    def term_copy(d):
        return copy_to(d, terms_ref.at[lax.rem(me + d, n)], back_ref.at[me], send_sem, recv_sem)

    def each(fn):
        def body(d, carry):
            fn(d)
            return carry
        lax.fori_loop(1, n, body, 0)

    if reduce_here:
        piece = grad_ref.shape[0] // n

        def part_copy(d):
            return copy_to(d, gstage.at[lax.rem(me + d, n)], gin.at[me], rsend, rrecv)

        def all_copy(d):
            return copy_to(d, gall.at[me], gall.at[me], asend, arecv)

        gstage[...] = grad_ref[...].astype(BF16).reshape(gstage.shape)
        each(lambda d: part_copy(d).start())
    each(lambda d: term_copy(d).start())
    back_ref[me] = terms_ref[me]
    if reduce_here:
        gin[me] = gstage[me]
        each(lambda d: part_copy(d).wait_recv())
        gall[me] = jnp.sum(gin[...].astype(F32), axis=0).astype(BF16)
        each(lambda d: all_copy(d).start())
    each(lambda d: term_copy(d).wait())
    if reduce_here:
        each(lambda d: part_copy(d).wait_send())
        each(lambda d: all_copy(d).wait())
        total = gall[...].astype(F32).reshape(grad_ref.shape) * factor
        half = total.shape[1] // 2
        total = jnp.where(feat == 0, total, jnp.concatenate([total[:, half:], total[:, :half]], axis=1))
        self_ref[...] = total[: self_ref.shape[0]]
        neigh_ref[...] = total[self_ref.shape[0]:]


def finish_kernel(hub_dev, send_ref, hub_ref, direct_ref, back_ref, out_ref):
    n = back_ref.shape[0]
    edge = 128
    out_ref[...] = direct_ref[...]

    def add(q, carry):
        rows = pl.ds(pl.multiple_of(send_ref[q] * edge, edge), edge)
        out_ref[rows, :] += back_ref[q, 0:edge, :].astype(F32)
        return carry

    lax.fori_loop(0, n, add, 0)

    def gather(q, total):
        return total + back_ref[q, edge:, :].astype(F32)

    total = lax.fori_loop(0, n, gather, jnp.zeros((back_ref.shape[1] - edge, back_ref.shape[2]), F32))
    for h in range(hub_dev):
        row = total[h:h + 1] + total[hub_dev + h:hub_dev + h + 1]
        out_ref[pl.ds(hub_ref[h], 1), :] += row


def shards(
    features, self_weight, neighbor_weight, tile_values, tile_row, tile_owner,
    send_tile, tile_count, hub_panel, hub_rows, cotangent,
):
    rows, half = features.shape
    edge = tile_values.shape[1]
    tiles = rows // edge
    n = lax.axis_size("dom")
    hub_dev = hub_rows.shape[0]
    hubs = hub_panel.shape[1]
    wide = 2 * half
    pad = -(-2 * hub_dev // 16) * 16
    tall = edge + pad
    sds = jax.ShapeDtypeStruct
    dma = pltpu.SemaphoreType.DMA
    params = functools.partial(pltpu.CompilerParams, vmem_limit_bytes=VMEM_BYTES)

    cols, x_all, c_all, ws_other, wn_other = pl.pallas_call(
        functools.partial(exchange_kernel, n, hub_dev),
        out_shape=(
            sds((n, tall, wide), BF16), sds((tiles, edge, wide), BF16), sds((tiles, edge, wide), BF16),
            sds(self_weight.shape, BF16), sds(neighbor_weight.shape, BF16),
        ),
        in_specs=[vmem()] * 4 + [smem()] * 2,
        out_specs=(vmem(),) * 5,
        scratch_shapes=[
            pltpu.VMEM((n, tall, half), BF16),
            dma((n,)), dma((n,)), dma((n,)), dma((n,)), dma((2,)), dma((4,)), dma((4,)),
        ],
        compiler_params=params(collective_id=0, has_side_effects=True),
        name="exchange",
    )(
        features.reshape(tiles, edge, half), cotangent.reshape(tiles, edge, half),
        self_weight, neighbor_weight, send_tile, hub_rows,
    )

    feat_index = lax.axis_index("feat").astype(jnp.int32).reshape(1)
    layer, grads, direct, terms = pl.pallas_call(
        functools.partial(local_kernel, hub_dev),
        out_shape=(
            sds((tiles, edge, half), BF16), sds((wide, wide), F32),
            sds((tiles, edge, half), F32), sds((n, tall, half), BF16),
        ),
        in_specs=[smem()] * 4 + [vmem()] * 9,
        out_specs=(vmem(),) * 4,
        scratch_shapes=[
            pltpu.VMEM((tiles, edge, wide), F32),
            pltpu.VMEM((tiles, edge, edge), F32),
            pltpu.VMEM((tiles, half, edge), BF16),
            pltpu.VMEM((n, half, edge), F32),
            pltpu.VMEM((half, hubs), F32),
        ],
        compiler_params=params(),
        name="local_pass",
    )(
        feat_index, tile_row, tile_owner, tile_count, cols, x_all, c_all,
        self_weight, neighbor_weight, ws_other, wn_other, tile_values,
        hub_panel.reshape(tiles, edge, hubs),
    )

    factor = 1.0 / math.sqrt(rows * n)
    reduce_here = wide % (16 * n) == 0
    back_shape = sds((n, tall, half), BF16)
    if reduce_here:
        part = (n, wide // n, wide)
        back, self_grad, neighbor_grad = pl.pallas_call(
            functools.partial(return_kernel, n, True, factor),
            out_shape=(back_shape, sds((half, wide), F32), sds((half, wide), F32)),
            in_specs=[vmem()] * 2,
            out_specs=(vmem(),) * 3,
            scratch_shapes=[dma((n,)), dma((n,))] + [pltpu.VMEM(part, BF16)] * 3 + [dma((n,))] * 4,
            compiler_params=params(collective_id=1, has_side_effects=True),
            name="send_back",
        )(terms, grads)
    else:
        back = pl.pallas_call(
            functools.partial(return_kernel, n, False, factor),
            out_shape=back_shape,
            in_specs=[vmem()],
            out_specs=vmem(),
            scratch_shapes=[dma((n,)), dma((n,))],
            compiler_params=params(collective_id=1, has_side_effects=True),
            name="send_back",
        )(terms)
        total = lax.psum(grads, "dom") * factor
        swapped = jnp.concatenate([total[:, half:], total[:, :half]], axis=1)
        total = jnp.where(feat_index[0] == 0, total, swapped)
        self_grad, neighbor_grad = total[:half], total[half:]

    input_grad = pl.pallas_call(
        functools.partial(finish_kernel, hub_dev),
        out_shape=sds((rows, half), F32),
        in_specs=[smem()] * 2 + [vmem()] * 2,
        out_specs=vmem(),
        compiler_params=params(),
        name="finish",
    )(send_tile, hub_rows, direct.reshape(rows, half), back)
    return layer.reshape(rows, half), self_grad, neighbor_grad, input_grad


def solution(mesh):
    placed = (
        P("dom", "feat"), P("feat", None), P("feat", None), P("dom", None, None), P("dom"), P("dom"),
        P("dom"), P("dom"), P("dom", None), P("dom"), P("dom", "feat"),
    )
    return jax.shard_map(
        shards,
        mesh=mesh,
        in_specs=placed,
        out_specs=(P("dom", "feat"), P("feat", None), P("feat", None), P("dom", "feat")),
        check_vma=False,
    )
```

time: 362 us -> 110 us (0.30)
  blocking collectives: 120 us -> 0 us
  Pallas kernels: 0 us -> 104 us
  other arithmetic: 66.9 us -> 0 us
  waiting for transfers between devices: 47.5 us -> 0 us
  local copies, waits for them, and re-layouts: 50.4 us -> 3.58 us
  matrix products: 44.7 us -> 0 us
  starting transfers between devices: 15.7 us -> 0 us
  between operations: 15.3 us -> 1.32 us
    pallas_call x0 -> x4, Pallas kernels: none -> 104 us  [the longest x1 39.7 us: shards(): pl.pallas_call(functools.partial(return_kernel, n, True, factor), out_sha...]
    unnamed x1 -> x0, blocking collectives: 77.2 us -> none
    scatter-add x5 -> x0, other arithmetic: 51.1 us -> none  [the longest x1 21.2 us: shards(): jax.ops.segment_sum(tile_back, tile_owner, num_segments=dom_size)]
    dot_general x10 -> x0, matrix products: 44.7 us -> none  [the longest x1 11.9 us: shards(): jnp.einsum('kij,kjf->kif', tile_values, columns, preferred_element_type=j...]
    all_gather x1 -> x0, blocking collectives: 42.5 us -> none  [shards(): hub_feats = lax.all_gather(hub_local, 'dom', axis=0, tiled=True)]
    psum x1 -> x0, waiting for transfers between devices: 32.1 us -> none  [shards(): self_sum, neighbor_sum = lax.psum((self_term, neighbor_term), 'dom')]
    mul x2 -> x0, local copies, waits for them, and re-layouts: 23.5 us -> none  [the longest x1 11.8 us: shards(): jnp.einsum('kji,kjf->kif', tile_values, slope_tiles, preferred_element_ty...]
    gather x4 -> x0, local copies, waits for them, and re-layouts: 17.6 us -> none  [the longest x1 8.02 us: shards(): slope_tiles = agg_slopes.reshape(tiles_dev, tile_edge, half_width)[tile_row]]
  transfers between devices with their start and end apart: 5 -> 0, of which waited for: 3 -> 0; matrix products, arithmetic and copies ran while one was open for 6% -> 0% of each run, Pallas kernels for 0% -> 0%
where the time goes in v1:
time: 110 us; the launch traced here: 108 us
  Pallas kernels  104 us (95%)
  local copies, waits for them, and re-layouts  3.58 us (3%)
  between operations  1.32 us (1%)
    pallas_call x1, Pallas kernels, shards(): pl.pallas_call(functools.partial(return_kernel, n, True, factor), out_sha...  39.7 us
    pallas_call x1, Pallas kernels, shards(): pl.pallas_call(functools.partial(local_kernel, hub_dev), out_shape=(sds((...  38.5 us
    pallas_call x1, Pallas kernels, shards(): pl.pallas_call(functools.partial(exchange_kernel, n, hub_dev), out_shape=...  21.9 us
    unnamed x7, local copies, waits for them, and re-layouts  3.58 us
    pallas_call x1, Pallas kernels, shards(): pl.pallas_call(functools.partial(finish_kernel, hub_dev), out_shape=sds((...  3.47 us

profile of v1, /device:TPU:0, one launch (start us, length us, event | category | flops | bytes accessed | tf_op | source)
XLA Modules:
  0.0 108.5 jit_solution(1487371062831948492)
XLA Ops:
  1.3 2.3 %copy.15 = bf16[4096,32]{1,0:T(8,128)(2,1)} copy(bf16[4096,32]{0,1:T(8,128)(2,1)} %param.19) | data formatting | bytes 524288 | tf_op args[8]
  3.5 21.9 %exchange.1 = (bf16[16,144,256]{2,1,0:T(8,128)(2,1)}, bf16[32,128,256]{2,1,0:T(8,128)(2,1)}, bf16[32,128,256]{2,1,0:T(8,128)(2,1)}, bf16[128,256]{1,0:T(8,128)(2,1)}, bf16[128,256]{1,0:T(8,128)(2,1)}) custom-call(bf16[32,128,128]{2,1,0:T(8,128)(2,1)} %bitcast.8, bf16[32,128,128]{2,1,0:T(8,128)(2,1)} %bitcast.9, bf16[128,256]{1,0:T(8,128)(2,1)} %ws_ref.3, ...), custom_call_target="tpu_custom_call" | custom-call | tf_op jit(solution)/shard_map/exchange/pallas_call | solution.py:345
  25.4 38.5 %local_pass.1 = (bf16[32,128,128]{2,1,0:T(8,128)(2,1)}, f32[256,256]{1,0:T(8,128)}, f32[32,128,128]{2,1,0:T(8,128)}, bf16[16,144,128]{2,1,0:T(8,128)(2,1)}) custom-call(s32[1]{0:T(128)} %bitcast.feat_ref, s32[160]{0:T(256)} %row_ref.1, s32[160]{0:T(256)} %owner_ref.1, s32[1]{0:T(128)S(6)} %copy.18.count_ref, ...), custom_call_target="tpu_custom_call" | custom-call | tf_op jit(solution)/shard_map/local_pass/pallas_call | solution.py:365
  64.0 39.7 %send_back.1 = (bf16[16,144,128]{2,1,0:T(8,128)(2,1)}, f32[128,256]{1,0:T(8,128)}, f32[128,256]{1,0:T(8,128)}) custom-call(bf16[16,144,128]{2,1,0:T(8,128)(2,1)} %get-tuple-element.22.refs_0_, f32[256,256]{1,0:T(8,128)} %get-tuple-element.23.refs_1_), custom_call_target="tpu_custom_call" | custom-call | tf_op jit(solution)/shard_map/send_back/pallas_call | solution.py:393
  103.7 0.0 copy-start.1
  103.7 0.0 copy-start
  103.7 3.5 %finish.1 = f32[4096,128]{1,0:T(8,128)} custom-call(s32[16]{0:T(128)} %send_ref.3, s32[2]{0:T(128)} %hub_ref.3, f32[4096,128]{1,0:T(8,128)} %bitcast.7, bf16[16,144,128]{2,1,0:T(8,128)(2,1)} %get-tuple-element.27.back_ref), custom_call_target="tpu_custom_call" | custom-call | tf_op jit(solution)/shard_map/finish/pallas_call | solution.py:417
  107.1 0.0 copy-done.1
  107.1 0.7 copy.19
  107.8 0.0 copy-done
  107.8 0.7 copy.20
Async XLA Ops:
  103.7 3.5 %copy-start.1 = (f32[128,256]{1,0:T(8,128)S(1)}, f32[128,256]{1,0:T(8,128)}, u32[]{:S(2)}) copy-start(f32[128,256]{1,0:T(8,128)} %get-tuple-element.33) | copy-start | bytes 393220
  103.7 4.1 %copy-start = (f32[128,256]{1,0:T(8,128)S(1)}, f32[128,256]{1,0:T(8,128)}, u32[]{:S(2)}) copy-start(f32[128,256]{1,0:T(8,128)} %get-tuple-element.34) | copy-start | bytes 393220

commit v2 on v1

--- a/solution.py
+++ b/solution.py
@@ -11,7 +11,7 @@
 F32 = jnp.float32
 BF16 = jnp.bfloat16
 VMEM_BYTES = 58 * 2**20
-UNROLL = 4
+UNROLL = 8
 
 
 def vmem():
@@ -135,12 +135,12 @@
     lax.fori_loop(0, n, finish_forward, 0)
 
 
-def slot_loop(count, step):
-    full = count // UNROLL
+def slot_loop(first, last, step):
+    full = (last - first) // UNROLL
 
     def many(i, carry):
         for u in range(UNROLL):
-            step(i * UNROLL + u)
+            step(first + i * UNROLL + u)
         return carry
 
     lax.fori_loop(0, full, many, 0)
@@ -149,30 +149,56 @@
         step(k)
         return carry
 
-    lax.fori_loop(full * UNROLL, count, single, 0)
+    lax.fori_loop(first + full * UNROLL, last, single, 0)
 
 
 def local_kernel(
     hub_dev, feat_ref, row_ref, owner_ref, count_ref,
-    cols_ref, x_ref, c_ref, ws_ref, wn_ref, wso_ref, wno_ref, val_ref, panel_ref,
-    out_ref, grad_ref, direct_ref, terms_ref,
-    acc, sq, slopes_t, terms_t, hub_s,
+    cols_ref, x_hbm, c_hbm, ws_ref, wn_ref, wso_ref, wno_ref, val_hbm, panel_ref,
+    out_hbm, grad_ref, direct_hbm, terms_ref,
+    acc, sq, slopes_t, terms_t, hub_s, x_ref, c_ref, val_ref, out_ref, direct_ref, w_ahead, w_back,
+    val_sem, in_sem, out_sem, direct_sem,
 ):
     f = feat_ref[0]
     tiles, edge, wide = x_ref.shape
     half = wide // 2
     n = cols_ref.shape[0]
-    hubs = panel_ref.shape[2]
+    hubs = panel_ref.shape[0]
     pad = cols_ref.shape[1] - edge
+    parts = val_sem.shape[0]
+    cap = val_ref.shape[0] // parts
+    group = tiles // out_sem.shape[0]
+    rows = group * edge
     count = count_ref[0]
+
+    def val_copy(i):
+        return pltpu.make_async_copy(
+            val_hbm.at[pl.ds(i * cap, cap)], val_ref.at[pl.ds(i * cap, cap)], val_sem.at[i]
+        )
+
+    def out_copies(i):
+        span = pl.ds(i * group, group)
+        return (
+            pltpu.make_async_copy(out_ref.at[span], out_hbm.at[span], out_sem.at[i]),
+            pltpu.make_async_copy(direct_ref.at[span], direct_hbm.at[span], direct_sem.at[i]),
+        )
+
+    for i in range(parts):
+        val_copy(i).start()
+    x_copy = pltpu.make_async_copy(x_hbm, x_ref, in_sem.at[0])
+    c_copy = pltpu.make_async_copy(c_hbm, c_ref, in_sem.at[1])
+    x_copy.start()
+    c_copy.start()
 
     def local_order(w):
         return jnp.where(f == 0, w, jnp.concatenate([w[:, half:], w[:, :half]], axis=1))
 
-    ws_own = local_order(ws_ref[...].astype(F32)).astype(BF16)
-    wn_own = local_order(wn_ref[...].astype(F32)).astype(BF16)
-    ws_all = jnp.concatenate([ws_own, local_order(wso_ref[...].astype(F32)).astype(BF16)], axis=0)
-    wn_all = jnp.concatenate([wn_own, local_order(wno_ref[...].astype(F32)).astype(BF16)], axis=0)
+    ws_own = local_order(ws_ref[...].astype(F32))
+    wn_own = local_order(wn_ref[...].astype(F32))
+    ws_other = local_order(wso_ref[...].astype(F32))
+    wn_other = local_order(wno_ref[...].astype(F32))
+    w_ahead[...] = jnp.concatenate([ws_own, ws_other, wn_own, wn_other], axis=0).astype(BF16)
+    w_back[...] = jnp.concatenate([ws_own, wn_own], axis=0).T.astype(BF16)
 
     hub_ids = lax.broadcasted_iota(jnp.int32, (hubs, n * pad), 0)
     place = lax.broadcasted_iota(jnp.int32, (hubs, n * pad), 1)
@@ -180,13 +206,22 @@
     hub_rows = cols_ref[:, edge:, :].reshape(n * pad, wide)
     hub_feats = dot(jnp.where(pick, 1.0, 0.0).astype(BF16), hub_rows).astype(BF16)
 
-    def start(t, carry):
-        panel = panel_ref[t]
-        acc[t] = dot(panel, hub_feats)
-        sq[t] = jnp.zeros((edge, edge), F32)
-        return carry
-
-    lax.fori_loop(0, tiles, start, 0)
+    def panel_part(i):
+        return panel_ref[:, pl.ds(pl.multiple_of(i * rows, rows), rows)]
+
+    def start(i, carry):
+        panel = panel_part(i).astype(F32).T
+        span = pl.ds(i * group, group)
+        acc[span] = dot(panel.astype(BF16), hub_feats).reshape(group, edge, wide)
+        squares = panel * panel
+        if hubs < edge:
+            squares = jnp.concatenate([squares, jnp.zeros((rows, edge - hubs), F32)], axis=1)
+        else:
+            squares = sum(squares[:, j:j + edge] for j in range(0, hubs, edge))
+        sq[span] = squares.reshape(group, edge, edge)
+        return carry
+
+    lax.fori_loop(0, tiles // group, start, 0)
 
     def ahead(k):
         values = val_ref[k]
@@ -195,31 +230,47 @@
         wide_values = values.astype(F32)
         sq[row] += wide_values * wide_values
 
-    slot_loop(count, ahead)
+    def part(i, carry):
+        val_copy(i).wait()
+        first = i * cap
+        slot_loop(first, jnp.clip(count, first, first + cap), ahead)
+        return carry
+
+    lax.fori_loop(0, parts, part, 0)
 
     grad_ref[...] = jnp.zeros_like(grad_ref)
     hub_s[...] = jnp.zeros_like(hub_s)
-
-    def dense(t, carry):
-        panel = panel_ref[t]
-        wide_panel = panel.astype(F32)
-        squares = jnp.sum(sq[t], axis=1, keepdims=True) + jnp.sum(wide_panel * wide_panel, axis=1, keepdims=True)
-        inverse = lax.rsqrt(1.0 + squares)
-        aggregate = (acc[t] * inverse).astype(BF16)
-        x = x_ref[t]
-        preact = dot(x, ws_all) + dot(aggregate, wn_all)
-        out_ref[t] = jnp.maximum(preact[:, :half], 0.0).astype(BF16)
-        slopes = jnp.where(preact > 0, c_ref[t].astype(F32), 0.0).astype(BF16)
-        direct_ref[t] = dot(slopes, ws_own, ((1,), (1,)))
-        back = dot(slopes, wn_own, ((1,), (1,))) * inverse
-        back_t = back.T.astype(BF16)
-        slopes_t[t] = back_t
-        hub_s[...] += dot(back_t, panel)
+    ones = jnp.ones((2 * edge, half), BF16)
+    x_copy.wait()
+    c_copy.wait()
+
+    def dense(i, carry):
+        span = pl.ds(i * group, group)
+        squares = sq[span].reshape(rows, edge)
+        high = squares.astype(BF16)
+        low = (squares - high.astype(F32)).astype(BF16)
+        inverse = lax.rsqrt(1.0 + dot(jnp.concatenate([high, low], axis=1), ones))
+        x = x_ref[span].reshape(rows, wide)
+        sums = acc[span].reshape(rows, wide)
+        aggregate = (sums * jnp.concatenate([inverse, inverse], axis=1)).astype(BF16)
+        preact = dot(jnp.concatenate([x, aggregate], axis=1), w_ahead[...])
+        out_ref[span] = jnp.maximum(preact[:, :half], 0.0).astype(BF16).reshape(group, edge, half)
+        cotangent = c_ref[span].reshape(rows, wide).astype(F32)
+        slopes = jnp.where(preact > 0, cotangent, 0.0).astype(BF16)
+        both = dot(slopes, w_back[...])
+        direct_ref[span] = both[:, :half].reshape(group, edge, half)
+        for copy in out_copies(i):
+            copy.start()
+        back = (both[:, half:] * inverse).astype(BF16)
+        hub_s[...] += dot(panel_part(i), back)
+        back_t = back.T
+        for g in range(group):
+            slopes_t[i * group + g] = back_t[:, g * edge:(g + 1) * edge]
         left = jnp.concatenate([x[:, :half], aggregate[:, :half]], axis=1)
         grad_ref[...] += dot(left, slopes, ((0,), (0,)))
         return carry
 
-    lax.fori_loop(0, tiles, dense, 0)
+    lax.fori_loop(0, tiles // group, dense, 0)
 
     def clear(o, carry):
         terms_t[o] = jnp.zeros((half, edge), F32)
@@ -230,9 +281,9 @@
     def behind(k):
         terms_t[owner_ref[k]] += dot(slopes_t[row_ref[k]], val_ref[k])
 
-    slot_loop(count, behind)
-
-    hub_terms = hub_s[...].T
+    slot_loop(0, count, behind)
+
+    hub_terms = hub_s[...]
     high = hub_terms.astype(BF16)
     low = (hub_terms - high.astype(F32)).astype(BF16)
     ids = lax.broadcasted_iota(jnp.int32, (n * pad, hubs), 1)
@@ -248,6 +299,13 @@
         return carry
 
     lax.fori_loop(0, n, emit, 0)
+
+    def drain(i, carry):
+        for copy in out_copies(i):
+            copy.wait()
+        return carry
+
+    lax.fori_loop(0, tiles // group, drain, 0)
 
 
 def return_kernel(n, reduce_here, factor, *refs):
@@ -362,27 +420,38 @@
     )
 
     feat_index = lax.axis_index("feat").astype(jnp.int32).reshape(1)
+    anywhere = pl.BlockSpec(memory_space=pl.ANY)
+    slots = tile_values.shape[0]
+    parts = math.gcd(slots, 8)
+    chunks = tiles // math.gcd(tiles, 4)
     layer, grads, direct, terms = pl.pallas_call(
         functools.partial(local_kernel, hub_dev),
         out_shape=(
             sds((tiles, edge, half), BF16), sds((wide, wide), F32),
             sds((tiles, edge, half), F32), sds((n, tall, half), BF16),
         ),
-        in_specs=[smem()] * 4 + [vmem()] * 9,
-        out_specs=(vmem(),) * 4,
+        in_specs=[smem()] * 4 + [vmem(), anywhere, anywhere] + [vmem()] * 4 + [anywhere, vmem()],
+        out_specs=(anywhere, vmem(), anywhere, vmem()),
         scratch_shapes=[
             pltpu.VMEM((tiles, edge, wide), F32),
             pltpu.VMEM((tiles, edge, edge), F32),
             pltpu.VMEM((tiles, half, edge), BF16),
             pltpu.VMEM((n, half, edge), F32),
-            pltpu.VMEM((half, hubs), F32),
+            pltpu.VMEM((hubs, half), F32),
+            pltpu.VMEM((tiles, edge, wide), BF16),
+            pltpu.VMEM((tiles, edge, wide), BF16),
+            pltpu.VMEM(tile_values.shape, BF16),
+            pltpu.VMEM((tiles, edge, half), BF16),
+            pltpu.VMEM((tiles, edge, half), F32),
+            pltpu.VMEM((2 * wide, wide), BF16),
+            pltpu.VMEM((wide, wide), BF16),
+            dma((parts,)), dma((2,)), dma((chunks,)), dma((chunks,)),
         ],
         compiler_params=params(),
         name="local_pass",
     )(
         feat_index, tile_row, tile_owner, tile_count, cols, x_all, c_all,
-        self_weight, neighbor_weight, ws_other, wn_other, tile_values,
-        hub_panel.reshape(tiles, edge, hubs),
+        self_weight, neighbor_weight, ws_other, wn_other, tile_values, hub_panel.T,
     )
 
     factor = 1.0 / math.sqrt(rows * n)

time: 110 us -> 84.4 us (0.77); the launches traced: 108 us -> 85 us
  Pallas kernels: 104 us -> 82.4 us
  local copies, waits for them, and re-layouts: 3.58 us -> 1.32 us
    pallas_call x1, Pallas kernels: 38.5 us -> 20.7 us  [shards(): pl.pallas_call(functools.partial(local_kernel, hub_dev), out_shape=(sds((...]
    pallas_call x1, Pallas kernels: 39.7 us -> 36.4 us  [shards(): pl.pallas_call(functools.partial(return_kernel, n, True, factor), out_sha...]
    unnamed x7 -> x6, local copies, waits for them, and re-layouts: 3.58 us -> 1.32 us
where the time goes in v2:
time: 84.4 us; the launch traced here: 85 us
  Pallas kernels  82.4 us (98%)
  local copies, waits for them, and re-layouts  1.32 us (2%)
  between operations  1.32 us (2%)
    pallas_call x1, Pallas kernels, shards(): pl.pallas_call(functools.partial(return_kernel, n, True, factor), out_sha...  36.4 us
    pallas_call x1, Pallas kernels, shards(): pl.pallas_call(functools.partial(exchange_kernel, n, hub_dev), out_shape=...  21.8 us
    pallas_call x1, Pallas kernels, shards(): pl.pallas_call(functools.partial(local_kernel, hub_dev), out_shape=(sds((...  20.7 us
    pallas_call x1, Pallas kernels, shards(): pl.pallas_call(functools.partial(finish_kernel, hub_dev), out_shape=sds((...  3.47 us

profile of v2, /device:TPU:0, one launch (start us, length us, event | category | flops | bytes accessed | tf_op | source)
XLA Modules:
  0.0 85.0 jit_solution(9039322605869757643)
XLA Ops:
  1.3 21.8 %exchange.1 = (bf16[16,144,256]{2,1,0:T(8,128)(2,1)}, bf16[32,128,256]{2,1,0:T(8,128)(2,1)}, bf16[32,128,256]{2,1,0:T(8,128)(2,1)}, bf16[128,256]{1,0:T(8,128)(2,1)}, bf16[128,256]{1,0:T(8,128)(2,1)}) custom-call(bf16[32,128,128]{2,1,0:T(8,128)(2,1)} %bitcast.7, bf16[32,128,128]{2,1,0:T(8,128)(2,1)} %bitcast.8, bf16[128,256]{1,0:T(8,128)(2,1)} %ws_ref.3, ...), custom_call_target="tpu_custom_call" | custom-call | tf_op jit(solution)/shard_map/exchange/pallas_call | solution.py:403
  23.1 20.7 %local_pass.1 = (bf16[32,128,128]{2,1,0:T(8,128)(2,1)}, f32[256,256]{1,0:T(8,128)}, f32[32,128,128]{2,1,0:T(8,128)}, bf16[16,144,128]{2,1,0:T(8,128)(2,1)}) custom-call(s32[1]{0:T(128)} %bitcast.feat_ref, s32[160]{0:T(256)} %row_ref.1, s32[160]{0:T(256)} %owner_ref.1, s32[1]{0:T(128)S(6)} %copy.17.count_ref, ...), custom_call_target="tpu_custom_call" | custom-call | tf_op jit(solution)/shard_map/local_pass/pallas_call | solution.py:427
  43.8 36.4 %send_back.1 = (bf16[16,144,128]{2,1,0:T(8,128)(2,1)}, f32[128,256]{1,0:T(8,128)}, f32[128,256]{1,0:T(8,128)}) custom-call(bf16[16,144,128]{2,1,0:T(8,128)(2,1)} %get-tuple-element.22.refs_0_, f32[256,256]{1,0:T(8,128)} %get-tuple-element.23.refs_1_), custom_call_target="tpu_custom_call" | custom-call | tf_op jit(solution)/shard_map/send_back/pallas_call | solution.py:462
  80.2 0.0 copy-start.1
  80.2 0.0 copy-start
  80.2 3.5 %finish.1 = f32[4096,128]{1,0:T(8,128)} custom-call(s32[16]{0:T(128)} %send_ref.3, s32[2]{0:T(128)} %hub_ref.3, f32[4096,128]{1,0:T(8,128)} %bitcast.6, bf16[16,144,128]{2,1,0:T(8,128)(2,1)} %get-tuple-element.27.back_ref), custom_call_target="tpu_custom_call" | custom-call | tf_op jit(solution)/shard_map/finish/pallas_call | solution.py:486
  83.7 0.0 copy-done.1
  83.7 0.7 copy.18
  84.4 0.0 copy-done
  84.4 0.7 copy.19
Async XLA Ops:
  80.2 3.5 %copy-start.1 = (f32[128,256]{1,0:T(8,128)S(1)}, f32[128,256]{1,0:T(8,128)}, u32[]{:S(2)}) copy-start(f32[128,256]{1,0:T(8,128)} %get-tuple-element.33) | copy-start | bytes 393220
  80.2 4.1 %copy-start = (f32[128,256]{1,0:T(8,128)S(1)}, f32[128,256]{1,0:T(8,128)}, u32[]{:S(2)}) copy-start(f32[128,256]{1,0:T(8,128)} %get-tuple-element.34) | copy-start | bytes 393220

commit v3 on v2

--- a/solution.py
+++ b/solution.py
@@ -38,7 +38,10 @@
     lax.fori_loop(1, n, hello, 0)
     if with_sibling:
         pl.semaphore_signal(barrier, inc=1, device_id={"feat": 1 - feat}, device_id_type=pl.DeviceIdType.MESH)
-    pl.semaphore_wait(barrier, n if with_sibling else n - 1)
+
+
+def wait_greetings(count):
+    pl.semaphore_wait(pltpu.get_barrier_semaphore(), count)
 
 
 def exchange_kernel(
@@ -64,6 +67,16 @@
         hub_block = jnp.where(out_ids == h, row, hub_block)
     hub_block = hub_block.astype(BF16)
 
+    def fill(d, carry):
+        stage[d, 0:edge, :] = feat_ref[send_ref[lax.rem(me + d, n)]]
+        stage[d, edge:, :] = hub_block
+        return carry
+
+    lax.fori_loop(1, n, fill, 0)
+    cols_ref[me, 0:edge, 0:half] = feat_ref[send_ref[me]]
+    cols_ref[me, edge:, 0:half] = hub_block
+    wait_greetings(n)
+
     def peer_copy(d):
         return pltpu.make_async_remote_copy(
             src_ref=stage.at[d], dst_ref=cols_ref.at[me, :, 0:half],
@@ -79,15 +92,10 @@
         )
 
     def send(d, carry):
-        q = lax.rem(me + d, n)
-        stage[d, 0:edge, :] = feat_ref[send_ref[q]]
-        stage[d, edge:, :] = hub_block
         peer_copy(d).start()
         return carry
 
     lax.fori_loop(1, n, send, 0)
-    cols_ref[me, 0:edge, 0:half] = feat_ref[send_ref[me]]
-    cols_ref[me, edge:, 0:half] = hub_block
     forward(me).start()
 
     extras = [
@@ -308,53 +316,79 @@
     lax.fori_loop(0, tiles // group, drain, 0)
 
 
-def return_kernel(n, reduce_here, factor, *refs):
-    if reduce_here:
+def return_kernel(n, inner, factor, *refs):
+    if inner:
         (terms_ref, grad_ref, back_ref, self_ref, neigh_ref,
-         send_sem, recv_sem, gstage, gin, gall, rsend, rrecv, asend, arecv) = refs
+         send_sem, recv_sem, gstage, gin, hstage, hin, gall, step_send, step_recv) = refs
     else:
         terms_ref, back_ref, send_sem, recv_sem = refs
     me = lax.axis_index("dom")
     feat = lax.axis_index("feat")
     greet(n, me, feat, False)
-
-    def copy_to(d, src, dst, ssem, rsem):
+    if inner:
+        gstage[...] = grad_ref[...].astype(BF16).reshape(gstage.shape)
+    back_ref[me] = terms_ref[me]
+    wait_greetings(n - 1)
+
+    def copy_to(target, src, dst, ssem, rsem):
         return pltpu.make_async_remote_copy(
-            src_ref=src, dst_ref=dst, send_sem=ssem.at[d], recv_sem=rsem.at[d],
-            device_id={"dom": lax.rem(me + d, n)}, device_id_type=pl.DeviceIdType.MESH,
+            src_ref=src, dst_ref=dst, send_sem=ssem, recv_sem=rsem,
+            device_id={"dom": target}, device_id_type=pl.DeviceIdType.MESH,
         )
 
     def term_copy(d):
-        return copy_to(d, terms_ref.at[lax.rem(me + d, n)], back_ref.at[me], send_sem, recv_sem)
-
-    def each(fn):
+        q = lax.rem(me + d, n)
+        return copy_to(q, terms_ref.at[q], back_ref.at[me], send_sem.at[d], recv_sem.at[d])
+
+    def each(fn, size):
         def body(d, carry):
             fn(d)
             return carry
-        lax.fori_loop(1, n, body, 0)
-
-    if reduce_here:
-        piece = grad_ref.shape[0] // n
-
-        def part_copy(d):
-            return copy_to(d, gstage.at[lax.rem(me + d, n)], gin.at[me], rsend, rrecv)
-
-        def all_copy(d):
-            return copy_to(d, gall.at[me], gall.at[me], asend, arecv)
-
-        gstage[...] = grad_ref[...].astype(BF16).reshape(gstage.shape)
-        each(lambda d: part_copy(d).start())
-    each(lambda d: term_copy(d).start())
-    back_ref[me] = terms_ref[me]
-    if reduce_here:
-        gin[me] = gstage[me]
-        each(lambda d: part_copy(d).wait_recv())
-        gall[me] = jnp.sum(gin[...].astype(F32), axis=0).astype(BF16)
-        each(lambda d: all_copy(d).start())
-    each(lambda d: term_copy(d).wait())
-    if reduce_here:
-        each(lambda d: part_copy(d).wait_send())
-        each(lambda d: all_copy(d).wait())
+        lax.fori_loop(1, size, body, 0)
+
+    if inner:
+        outer = n // inner
+        z, i = me // inner, lax.rem(me, inner)
+
+        def plane_copy(d, phase, src, dst):
+            j = lax.rem(i + d, inner)
+            return copy_to(z * inner + j, src(j), dst, step_send.at[phase, d], step_recv.at[phase, d])
+
+        def line_copy(d, phase, src, dst):
+            k = lax.rem(z + d, outer)
+            return copy_to(k * inner + i, src(k), dst, step_send.at[phase, d], step_recv.at[phase, d])
+
+        def scatter_plane(d):
+            return plane_copy(d, 0, lambda j: gstage.at[j], gin.at[i])
+
+        def scatter_line(d):
+            return line_copy(d, 1, lambda k: hstage.at[k], hin.at[z])
+
+        def gather_line(d):
+            return line_copy(d, 2, lambda k: gall.at[i, z], gall.at[i, z])
+
+        def gather_plane(d):
+            return plane_copy(d, 3, lambda j: gall.at[i], gall.at[i])
+
+        each(lambda d: scatter_plane(d).start(), inner)
+    each(lambda d: term_copy(d).start(), n)
+    if inner:
+        gin[i] = gstage[i]
+        each(lambda d: scatter_plane(d).wait_recv(), inner)
+        hstage[...] = jnp.sum(gin[...].astype(F32), axis=0).astype(BF16)
+        each(lambda d: scatter_line(d).start(), outer)
+        hin[z] = hstage[z]
+        each(lambda d: scatter_line(d).wait_recv(), outer)
+        gall[i, z] = jnp.sum(hin[...].astype(F32), axis=0).astype(BF16)
+        each(lambda d: gather_line(d).start(), outer)
+        each(lambda d: gather_line(d).wait_recv(), outer)
+        each(lambda d: gather_plane(d).start(), inner)
+    each(lambda d: term_copy(d).wait(), n)
+    if inner:
+        each(lambda d: scatter_plane(d).wait_send(), inner)
+        each(lambda d: scatter_line(d).wait_send(), outer)
+        each(lambda d: gather_line(d).wait_send(), outer)
+        each(lambda d: gather_plane(d).wait(), inner)
         total = gall[...].astype(F32).reshape(grad_ref.shape) * factor
         half = total.shape[1] // 2
         total = jnp.where(feat == 0, total, jnp.concatenate([total[:, half:], total[:, :half]], axis=1))
@@ -362,25 +396,31 @@
         neigh_ref[...] = total[self_ref.shape[0]:]
 
 
-def finish_kernel(hub_dev, send_ref, hub_ref, direct_ref, back_ref, out_ref):
+def finish_kernel(hub_dev, edge, send_ref, hub_ref, direct_ref, back_ref, out_ref):
     n = back_ref.shape[0]
-    edge = 128
+    span = out_ref.shape[0]
+    base = pl.program_id(0) * span
     out_ref[...] = direct_ref[...]
 
     def add(q, carry):
-        rows = pl.ds(pl.multiple_of(send_ref[q] * edge, edge), edge)
-        out_ref[rows, :] += back_ref[q, 0:edge, :].astype(F32)
+        place = send_ref[q] * edge - base
+
+        @pl.when((place >= 0) & (place < span))
+        def _():
+            rows = pl.ds(pl.multiple_of(place, edge), edge)
+            out_ref[rows, :] += back_ref[q, 0:edge, :].astype(F32)
+
         return carry
 
     lax.fori_loop(0, n, add, 0)
-
-    def gather(q, total):
-        return total + back_ref[q, edge:, :].astype(F32)
-
-    total = lax.fori_loop(0, n, gather, jnp.zeros((back_ref.shape[1] - edge, back_ref.shape[2]), F32))
     for h in range(hub_dev):
-        row = total[h:h + 1] + total[hub_dev + h:hub_dev + h + 1]
-        out_ref[pl.ds(hub_ref[h], 1), :] += row
+        place = hub_ref[h] - base
+
+        @pl.when((place >= 0) & (place < span))
+        def _():
+            total = jnp.sum(back_ref[:, edge:, :].astype(F32), axis=0)
+            row = total[h:h + 1] + total[hub_dev + h:hub_dev + h + 1]
+            out_ref[pl.ds(place, 1), :] += row
 
 
 def shards(
@@ -398,6 +438,7 @@
     tall = edge + pad
     sds = jax.ShapeDtypeStruct
     dma = pltpu.SemaphoreType.DMA
+    anywhere = pl.BlockSpec(memory_space=pl.ANY)
     params = functools.partial(pltpu.CompilerParams, vmem_limit_bytes=VMEM_BYTES)
 
     cols, x_all, c_all, ws_other, wn_other = pl.pallas_call(
@@ -406,8 +447,8 @@
             sds((n, tall, wide), BF16), sds((tiles, edge, wide), BF16), sds((tiles, edge, wide), BF16),
             sds(self_weight.shape, BF16), sds(neighbor_weight.shape, BF16),
         ),
-        in_specs=[vmem()] * 4 + [smem()] * 2,
-        out_specs=(vmem(),) * 5,
+        in_specs=[vmem(), anywhere, vmem(), vmem()] + [smem()] * 2,
+        out_specs=(vmem(), anywhere, anywhere, vmem(), vmem()),
         scratch_shapes=[
             pltpu.VMEM((n, tall, half), BF16),
             dma((n,)), dma((n,)), dma((n,)), dma((n,)), dma((2,)), dma((4,)), dma((4,)),
@@ -420,7 +461,6 @@
     )
 
     feat_index = lax.axis_index("feat").astype(jnp.int32).reshape(1)
-    anywhere = pl.BlockSpec(memory_space=pl.ANY)
     slots = tile_values.shape[0]
     parts = math.gcd(slots, 8)
     chunks = tiles // math.gcd(tiles, 4)
@@ -455,22 +495,30 @@
     )
 
     factor = 1.0 / math.sqrt(rows * n)
-    reduce_here = wide % (16 * n) == 0
+    inner = math.isqrt(n)
+    if inner * inner != n or wide % (16 * n):
+        inner = 0
     back_shape = sds((n, tall, half), BF16)
-    if reduce_here:
-        part = (n, wide // n, wide)
+    if inner:
+        line = (inner, wide // n, wide)
         back, self_grad, neighbor_grad = pl.pallas_call(
-            functools.partial(return_kernel, n, True, factor),
+            functools.partial(return_kernel, n, inner, factor),
             out_shape=(back_shape, sds((half, wide), F32), sds((half, wide), F32)),
             in_specs=[vmem()] * 2,
             out_specs=(vmem(),) * 3,
-            scratch_shapes=[dma((n,)), dma((n,))] + [pltpu.VMEM(part, BF16)] * 3 + [dma((n,))] * 4,
+            scratch_shapes=[
+                dma((n,)), dma((n,)),
+                pltpu.VMEM((inner,) + line, BF16), pltpu.VMEM((inner,) + line, BF16),
+                pltpu.VMEM(line, BF16), pltpu.VMEM(line, BF16),
+                pltpu.VMEM((inner,) + line, BF16),
+                dma((4, inner)), dma((4, inner)),
+            ],
             compiler_params=params(collective_id=1, has_side_effects=True),
             name="send_back",
         )(terms, grads)
     else:
         back = pl.pallas_call(
-            functools.partial(return_kernel, n, False, factor),
+            functools.partial(return_kernel, n, 0, factor),
             out_shape=back_shape,
             in_specs=[vmem()],
             out_specs=vmem(),
@@ -483,11 +531,14 @@
         total = jnp.where(feat_index[0] == 0, total, swapped)
         self_grad, neighbor_grad = total[:half], total[half:]
 
+    steps = math.gcd(tiles, 4)
+    block = pl.BlockSpec((rows // steps, half), lambda i: (i, 0))
     input_grad = pl.pallas_call(
-        functools.partial(finish_kernel, hub_dev),
+        functools.partial(finish_kernel, hub_dev, edge),
+        grid=(steps,),
         out_shape=sds((rows, half), F32),
-        in_specs=[smem()] * 2 + [vmem()] * 2,
-        out_specs=vmem(),
+        in_specs=[smem(), smem(), block, pl.BlockSpec((n, tall, half), lambda i: (0, 0, 0))],
+        out_specs=block,
         compiler_params=params(),
         name="finish",
     )(send_tile, hub_rows, direct.reshape(rows, half), back)

time: 84.4 us -> 104 us (1.23)
  Pallas kernels: 82.4 us -> 102 us
    pallas_call x1, Pallas kernels: 21.8 us -> 43.1 us  [shards(): pl.pallas_call(functools.partial(exchange_kernel, n, hub_dev), out_shape=...]
    pallas_call x2, Pallas kernels: 39.9 us -> 37.6 us  [the longest x1 33 us: shards(): pl.pallas_call(functools.partial(return_kernel, n, inner, factor), out_sh...]
where the time goes in v3:
time: 104 us
  Pallas kernels  102 us (98%)
  local copies, waits for them, and re-layouts  1.32 us (1%)
  between operations  1.32 us (1%)
    pallas_call x1, Pallas kernels, shards(): pl.pallas_call(functools.partial(exchange_kernel, n, hub_dev), out_shape=...  43.1 us
    pallas_call x1, Pallas kernels, shards(): pl.pallas_call(functools.partial(return_kernel, n, inner, factor), out_sh...  33 us
    pallas_call x1, Pallas kernels, shards(): pl.pallas_call(functools.partial(local_kernel, hub_dev), out_shape=(sds((...  21 us
    pallas_call x1, Pallas kernels, shards(): pl.pallas_call(functools.partial(finish_kernel, hub_dev, edge), grid=(ste...  4.65 us

profile of v3, /device:TPU:0, one launch (start us, length us, event | category | flops | bytes accessed | tf_op | source)
XLA Modules:
  0.0 104.3 jit_solution(12102317408339544564)
XLA Ops:
  1.3 43.1 %exchange.1 = (bf16[16,144,256]{2,1,0:T(8,128)(2,1)}, bf16[32,128,256]{2,1,0:T(8,128)(2,1)}, bf16[32,128,256]{2,1,0:T(8,128)(2,1)}, bf16[128,256]{1,0:T(8,128)(2,1)}, bf16[128,256]{1,0:T(8,128)(2,1)}) custom-call(bf16[32,128,128]{2,1,0:T(8,128)(2,1)} %bitcast.7, bf16[32,128,128]{2,1,0:T(8,128)(2,1)} %bitcast.8, bf16[128,256]{1,0:T(8,128)(2,1)} %ws_ref.3, ...), custom_call_target="tpu_custom_call" | custom-call | tf_op jit(solution)/shard_map/exchange/pallas_call | solution.py:444
  44.3 21.0 %local_pass.1 = (bf16[32,128,128]{2,1,0:T(8,128)(2,1)}, f32[256,256]{1,0:T(8,128)}, f32[32,128,128]{2,1,0:T(8,128)}, bf16[16,144,128]{2,1,0:T(8,128)(2,1)}) custom-call(s32[1]{0:T(128)} %bitcast.feat_ref, s32[160]{0:T(256)} %row_ref.1, s32[160]{0:T(256)} %owner_ref.1, s32[1]{0:T(128)S(6)} %copy.17.count_ref, ...), custom_call_target="tpu_custom_call" | custom-call | tf_op jit(solution)/shard_map/local_pass/pallas_call | solution.py:467
  65.3 33.0 %send_back.1 = (bf16[16,144,128]{2,1,0:T(8,128)(2,1)}, f32[128,256]{1,0:T(8,128)}, f32[128,256]{1,0:T(8,128)}) custom-call(bf16[16,144,128]{2,1,0:T(8,128)(2,1)} %get-tuple-element.22.refs_0_, f32[256,256]{1,0:T(8,128)} %get-tuple-element.23.refs_1_), custom_call_target="tpu_custom_call" | custom-call | tf_op jit(solution)/shard_map/send_back/pallas_call | solution.py:504
  98.3 0.0 copy-start.1
  98.3 0.0 copy-start
  98.3 4.6 %finish.1 = f32[4096,128]{1,0:T(8,128)} custom-call(s32[16]{0:T(128)} %send_ref.3, s32[2]{0:T(128)} %hub_ref.3, f32[4096,128]{1,0:T(8,128)} %bitcast.6, bf16[16,144,128]{2,1,0:T(8,128)(2,1)} %get-tuple-element.27.back_ref), custom_call_target="tpu_custom_call" | custom-call | tf_op jit(solution)/shard_map/finish/pallas_call | solution.py:536
  103.0 0.0 copy-done.1
  103.0 0.7 copy.18
  103.6 0.0 copy-done
  103.6 0.7 copy.19
Async XLA Ops:
  98.3 4.7 %copy-start.1 = (f32[128,256]{1,0:T(8,128)S(1)}, f32[128,256]{1,0:T(8,128)}, u32[]{:S(2)}) copy-start(f32[128,256]{1,0:T(8,128)} %get-tuple-element.33) | copy-start | bytes 393220
  98.3 5.3 %copy-start = (f32[128,256]{1,0:T(8,128)S(1)}, f32[128,256]{1,0:T(8,128)}, u32[]{:S(2)}) copy-start(f32[128,256]{1,0:T(8,128)} %get-tuple-element.34) | copy-start | bytes 393220

commit v4 on v2

--- a/solution.py
+++ b/solution.py
@@ -38,7 +38,14 @@
     lax.fori_loop(1, n, hello, 0)
     if with_sibling:
         pl.semaphore_signal(barrier, inc=1, device_id={"feat": 1 - feat}, device_id_type=pl.DeviceIdType.MESH)
-    pl.semaphore_wait(barrier, n if with_sibling else n - 1)
+
+
+def wait_greetings(count):
+    pl.semaphore_wait(pltpu.get_barrier_semaphore(), count)
+
+
+def far_first(k, n):
+    return lax.rem(n // 2 + lax.rem(k, 2) * (k + 1) // 2 - (1 - lax.rem(k, 2)) * (k // 2) + n, n)
 
 
 def exchange_kernel(
@@ -64,6 +71,16 @@
         hub_block = jnp.where(out_ids == h, row, hub_block)
     hub_block = hub_block.astype(BF16)
 
+    def fill(d, carry):
+        stage[d, 0:edge, :] = feat_ref[send_ref[lax.rem(me + d, n)]]
+        stage[d, edge:, :] = hub_block
+        return carry
+
+    lax.fori_loop(1, n, fill, 0)
+    cols_ref[me, 0:edge, 0:half] = feat_ref[send_ref[me]]
+    cols_ref[me, edge:, 0:half] = hub_block
+    wait_greetings(n)
+
     def peer_copy(d):
         return pltpu.make_async_remote_copy(
             src_ref=stage.at[d], dst_ref=cols_ref.at[me, :, 0:half],
@@ -78,16 +95,11 @@
             device_id={"feat": 1 - feat}, device_id_type=pl.DeviceIdType.MESH,
         )
 
-    def send(d, carry):
-        q = lax.rem(me + d, n)
-        stage[d, 0:edge, :] = feat_ref[send_ref[q]]
-        stage[d, edge:, :] = hub_block
-        peer_copy(d).start()
-        return carry
-
-    lax.fori_loop(1, n, send, 0)
-    cols_ref[me, 0:edge, 0:half] = feat_ref[send_ref[me]]
-    cols_ref[me, edge:, 0:half] = hub_block
+    def send(k, carry):
+        peer_copy(far_first(k, n)).start()
+        return carry
+
+    lax.fori_loop(0, n - 1, send, 0)
     forward(me).start()
 
     extras = [
@@ -308,15 +320,13 @@
     lax.fori_loop(0, tiles // group, drain, 0)
 
 
-def return_kernel(n, reduce_here, factor, *refs):
-    if reduce_here:
-        (terms_ref, grad_ref, back_ref, self_ref, neigh_ref,
-         send_sem, recv_sem, gstage, gin, gall, rsend, rrecv, asend, arecv) = refs
-    else:
-        terms_ref, back_ref, send_sem, recv_sem = refs
+def reduce_kernel(n, factor, grad_ref, self_ref, neigh_ref, gstage, gin, gall, rsend, rrecv, asend, arecv):
     me = lax.axis_index("dom")
     feat = lax.axis_index("feat")
     greet(n, me, feat, False)
+    gstage[...] = grad_ref[...].astype(BF16).reshape(gstage.shape)
+    gin[me] = gstage[me]
+    wait_greetings(n - 1)
 
     def copy_to(d, src, dst, ssem, rsem):
         return pltpu.make_async_remote_copy(
@@ -324,42 +334,29 @@
             device_id={"dom": lax.rem(me + d, n)}, device_id_type=pl.DeviceIdType.MESH,
         )
 
-    def term_copy(d):
-        return copy_to(d, terms_ref.at[lax.rem(me + d, n)], back_ref.at[me], send_sem, recv_sem)
+    def part_copy(d):
+        return copy_to(d, gstage.at[lax.rem(me + d, n)], gin.at[me], rsend, rrecv)
+
+    def all_copy(d):
+        return copy_to(d, gall.at[me], gall.at[me], asend, arecv)
 
     def each(fn):
-        def body(d, carry):
-            fn(d)
+        def body(k, carry):
+            fn(far_first(k, n))
             return carry
-        lax.fori_loop(1, n, body, 0)
-
-    if reduce_here:
-        piece = grad_ref.shape[0] // n
-
-        def part_copy(d):
-            return copy_to(d, gstage.at[lax.rem(me + d, n)], gin.at[me], rsend, rrecv)
-
-        def all_copy(d):
-            return copy_to(d, gall.at[me], gall.at[me], asend, arecv)
-
-        gstage[...] = grad_ref[...].astype(BF16).reshape(gstage.shape)
-        each(lambda d: part_copy(d).start())
-    each(lambda d: term_copy(d).start())
-    back_ref[me] = terms_ref[me]
-    if reduce_here:
-        gin[me] = gstage[me]
-        each(lambda d: part_copy(d).wait_recv())
-        gall[me] = jnp.sum(gin[...].astype(F32), axis=0).astype(BF16)
-        each(lambda d: all_copy(d).start())
-    each(lambda d: term_copy(d).wait())
-    if reduce_here:
-        each(lambda d: part_copy(d).wait_send())
-        each(lambda d: all_copy(d).wait())
-        total = gall[...].astype(F32).reshape(grad_ref.shape) * factor
-        half = total.shape[1] // 2
-        total = jnp.where(feat == 0, total, jnp.concatenate([total[:, half:], total[:, :half]], axis=1))
-        self_ref[...] = total[: self_ref.shape[0]]
-        neigh_ref[...] = total[self_ref.shape[0]:]
+        lax.fori_loop(0, n - 1, body, 0)
+
+    each(lambda d: part_copy(d).start())
+    each(lambda d: part_copy(d).wait_recv())
+    gall[me] = jnp.sum(gin[...].astype(F32), axis=0).astype(BF16)
+    each(lambda d: all_copy(d).start())
+    each(lambda d: part_copy(d).wait_send())
+    each(lambda d: all_copy(d).wait())
+    total = gall[...].astype(F32).reshape(grad_ref.shape) * factor
+    half = total.shape[1] // 2
+    total = jnp.where(feat == 0, total, jnp.concatenate([total[:, half:], total[:, :half]], axis=1))
+    self_ref[...] = total[: self_ref.shape[0]]
+    neigh_ref[...] = total[self_ref.shape[0]:]
 
 
 def finish_kernel(hub_dev, send_ref, hub_ref, direct_ref, back_ref, out_ref):
@@ -455,29 +452,20 @@
     )
 
     factor = 1.0 / math.sqrt(rows * n)
-    reduce_here = wide % (16 * n) == 0
-    back_shape = sds((n, tall, half), BF16)
-    if reduce_here:
+    back = lax.all_to_all(terms, "dom", split_axis=0, concat_axis=0, tiled=True)
+    if wide % (16 * n) == 0:
         part = (n, wide // n, wide)
-        back, self_grad, neighbor_grad = pl.pallas_call(
-            functools.partial(return_kernel, n, True, factor),
-            out_shape=(back_shape, sds((half, wide), F32), sds((half, wide), F32)),
-            in_specs=[vmem()] * 2,
-            out_specs=(vmem(),) * 3,
-            scratch_shapes=[dma((n,)), dma((n,))] + [pltpu.VMEM(part, BF16)] * 3 + [dma((n,))] * 4,
+        self_grad, neighbor_grad = pl.pallas_call(
+            functools.partial(reduce_kernel, n, factor),
+            out_shape=(sds((half, wide), F32), sds((half, wide), F32)),
+            in_specs=[vmem()],
+            out_specs=(vmem(),) * 2,
+            scratch_shapes=[pltpu.VMEM(part, BF16)] * 3 + [dma((n,))] * 4,
             compiler_params=params(collective_id=1, has_side_effects=True),
-            name="send_back",
-        )(terms, grads)
+            name="reduce_grads",
+            cost_estimate=pl.CostEstimate(flops=10**10, bytes_accessed=2**24, transcendentals=0),
+        )(grads)
     else:
-        back = pl.pallas_call(
-            functools.partial(return_kernel, n, False, factor),
-            out_shape=back_shape,
-            in_specs=[vmem()],
-            out_specs=vmem(),
-            scratch_shapes=[dma((n,)), dma((n,))],
-            compiler_params=params(collective_id=1, has_side_effects=True),
-            name="send_back",
-        )(terms)
         total = lax.psum(grads, "dom") * factor
         swapped = jnp.concatenate([total[:, half:], total[:, :half]], axis=1)
         total = jnp.where(feat_index[0] == 0, total, swapped)

time: 84.4 us -> 91.7 us (1.086)
  starting transfers between devices: 0 us -> 14.8 us
  Pallas kernels: 82.4 us -> 73.3 us
    all_to_all x0 -> x1, starting transfers between devices: none -> 14.8 us  [shards(): back = lax.all_to_all(terms, 'dom', split_axis=0, concat_axis=0, tiled=True)]
    pallas_call x1, Pallas kernels: 36.4 us -> 26.1 us  [shards(): pl.pallas_call(functools.partial(reduce_kernel, n, factor), out_shape=(sd...]
    pallas_call x1, Pallas kernels: 21.8 us -> 26.3 us  [shards(): pl.pallas_call(functools.partial(exchange_kernel, n, hub_dev), out_shape=...]
    pallas_call x1, Pallas kernels: 20.7 us -> 17.3 us  [shards(): pl.pallas_call(functools.partial(local_kernel, hub_dev), out_shape=(sds((...]
    unnamed x6 -> x8, local copies, waits for them, and re-layouts: 1.32 us -> 2.13 us
  transfers between devices with their start and end apart: 0 -> 1, of which waited for: 0 -> 0; matrix products, arithmetic and copies ran while one was open for 0% -> 0% of each run, Pallas kernels for 0% -> 29%
where the time goes in v4:
time: 91.7 us; the launch traced here: 91.6 us
  Pallas kernels  73.3 us (80%)
  starting transfers between devices  14.8 us (16%)
  local copies, waits for them, and re-layouts  2.13 us (2%)
  between operations  1.33 us (1%)
    pallas_call x1, Pallas kernels, shards(): pl.pallas_call(functools.partial(exchange_kernel, n, hub_dev), out_shape=...  26.3 us
    pallas_call x1, Pallas kernels, shards(): pl.pallas_call(functools.partial(reduce_kernel, n, factor), out_shape=(sd...  26.1 us
    pallas_call x1, Pallas kernels, shards(): pl.pallas_call(functools.partial(local_kernel, hub_dev), out_shape=(sds((...  17.3 us
    all_to_all x1, starting transfers between devices, shards(): back = lax.all_to_all(terms, 'dom', split_axis=0, concat_axis=0, tiled=True)  14.8 us
    pallas_call x1, Pallas kernels, shards(): pl.pallas_call(functools.partial(finish_kernel, hub_dev), out_shape=sds((...  3.47 us
    unnamed x8, local copies, waits for them, and re-layouts  2.13 us
  transfers between devices with their start and end apart: 1, of which 0 were waited for; matrix products, arithmetic and copies ran while one was open for 0% of the time, Pallas kernels for 29%

profile of v4, /device:TPU:0, one launch (start us, length us, event | category | flops | bytes accessed | tf_op | source)
XLA Modules:
  0.0 91.6 jit_solution(15251149970935834052)
XLA Ops:
  1.3 26.3 %exchange.1 = (bf16[16,144,256]{2,1,0:T(8,128)(2,1)}, bf16[32,128,256]{2,1,0:T(8,128)(2,1)}, bf16[32,128,256]{2,1,0:T(8,128)(2,1)}, bf16[128,256]{1,0:T(8,128)(2,1)}, bf16[128,256]{1,0:T(8,128)(2,1)}) custom-call(bf16[32,128,128]{2,1,0:T(8,128)(2,1)} %bitcast.7, bf16[32,128,128]{2,1,0:T(8,128)(2,1)} %bitcast.8, bf16[128,256]{1,0:T(8,128)(2,1)} %ws_ref.3, ...), custom_call_target="tpu_custom_call" | custom-call | tf_op jit(solution)/shard_map/exchange/pallas_call | solution.py:400
  27.6 17.3 %local_pass.1 = (bf16[32,128,128]{2,1,0:T(8,128)(2,1)}, f32[256,256]{1,0:T(8,128)}, f32[32,128,128]{2,1,0:T(8,128)}, bf16[16,144,128]{2,1,0:T(8,128)(2,1)}) custom-call(s32[1]{0:T(128)} %bitcast.feat_ref, s32[160]{0:T(256)} %row_ref.1, s32[160]{0:T(256)} %owner_ref.1, s32[1]{0:T(128)S(6)} %copy.17.count_ref, ...), custom_call_target="tpu_custom_call" | custom-call | tf_op jit(solution)/shard_map/local_pass/pallas_call | solution.py:424
  45.0 14.8 %all-to-all-start = ((bf16[16,144,128]{2,1,0:T(8,128)(2,1)}), bf16[16,144,128]{2,1,0:T(8,128)(2,1)S(1)}, u32[]{:S(2)}, u32[]{:S(2)}) async-start(bf16[16,144,128]{2,1,0:T(8,128)(2,1)} %get-tuple-element.25), calls=%async_computation | async-start | bytes 1179648 | tf_op jit(solution)/shard_map/all_to_all | solution.py:455
  59.8 26.1 %reduce_grads.1 = (f32[128,256]{1,0:T(8,128)}, f32[128,256]{1,0:T(8,128)}) custom-call(f32[256,256]{1,0:T(8,128)} %get-tuple-element.21.grad_ref), custom_call_target="tpu_custom_call" | custom-call | flops 10000000000 | bytes 16777216 | tf_op jit(solution)/shard_map/reduce_grads/pallas_call | solution.py:458
  86.0 0.0 all-to-all-done.back_ref
  86.0 0.0 copy-start
  86.0 0.8 copy-done
  86.8 0.0 copy-start.2
  86.8 0.0 copy-start.1
  86.8 3.5 %finish.1 = f32[4096,128]{1,0:T(8,128)} custom-call(s32[16]{0:T(128)} %send_ref.3, s32[2]{0:T(128)} %hub_ref.3, f32[4096,128]{1,0:T(8,128)} %bitcast.6, bf16[16,144,128]{2,1,0:T(8,128)(2,1)} %copy-done), custom_call_target="tpu_custom_call" | custom-call | tf_op jit(solution)/shard_map/finish/pallas_call | solution.py:474
  90.3 0.0 copy-done.2
  90.3 0.7 copy.18
  90.9 0.0 copy-done.1
  90.9 0.7 copy.19
Async XLA Ops:
  45.0 41.0 %all-to-all-start = ((bf16[16,144,128]{2,1,0:T(8,128)(2,1)}), bf16[16,144,128]{2,1,0:T(8,128)(2,1)S(1)}, u32[]{:S(2)}, u32[]{:S(2)}) async-start(bf16[16,144,128]{2,1,0:T(8,128)(2,1)} %get-tuple-element.25), calls=%async_computation | async-start | bytes 1179648 | tf_op jit(solution)/shard_map/all_to_all | solution.py:455
  86.0 0.8 copy-start
  86.8 3.5 %copy-start.2 = (f32[128,256]{1,0:T(8,128)S(1)}, f32[128,256]{1,0:T(8,128)}, u32[]{:S(2)}) copy-start(f32[128,256]{1,0:T(8,128)} %get-tuple-element.31) | copy-start | bytes 393220
  86.8 4.1 %copy-start.1 = (f32[128,256]{1,0:T(8,128)S(1)}, f32[128,256]{1,0:T(8,128)}, u32[]{:S(2)}) copy-start(f32[128,256]{1,0:T(8,128)} %get-tuple-element.32) | copy-start | bytes 393220

commit v5 on v3

--- a/solution.py
+++ b/solution.py
@@ -42,6 +42,10 @@
 
 def wait_greetings(count):
     pl.semaphore_wait(pltpu.get_barrier_semaphore(), count)
+
+
+def mixed(k, n):
+    return 1 + lax.rem(k * (n // 2 - 1), n - 1)
 
 
 def exchange_kernel(
@@ -91,11 +95,11 @@
             device_id={"feat": 1 - feat}, device_id_type=pl.DeviceIdType.MESH,
         )
 
-    def send(d, carry):
-        peer_copy(d).start()
-        return carry
-
-    lax.fori_loop(1, n, send, 0)
+    def send(k, carry):
+        peer_copy(mixed(k, n)).start()
+        return carry
+
+    lax.fori_loop(0, n - 1, send, 0)
     forward(me).start()
 
     extras = [
@@ -119,12 +123,13 @@
     for copy in locals_:
         copy.start()
 
-    def arrive(d, carry):
+    def arrive(k, carry):
+        d = mixed(k, n)
         peer_copy(d).wait_recv()
         forward(lax.rem(me - d + n, n)).start()
         return carry
 
-    lax.fori_loop(1, n, arrive, 0)
+    lax.fori_loop(0, n - 1, arrive, 0)
     for copy in locals_:
         copy.wait()
     for copy in extras:
@@ -340,6 +345,14 @@
         q = lax.rem(me + d, n)
         return copy_to(q, terms_ref.at[q], back_ref.at[me], send_sem.at[d], recv_sem.at[d])
 
+    def send_terms(first, last):
+        def body(k, carry):
+            term_copy(mixed(k, n)).start()
+            return carry
+        lax.fori_loop(first, last, body, 0)
+
+    batch = -(-(n - 1) // 3)
+
     def each(fn, size):
         def body(d, carry):
             fn(d)
@@ -371,18 +384,21 @@
             return plane_copy(d, 3, lambda j: gall.at[i], gall.at[i])
 
         each(lambda d: scatter_plane(d).start(), inner)
-    each(lambda d: term_copy(d).start(), n)
-    if inner:
+        send_terms(0, batch)
         gin[i] = gstage[i]
         each(lambda d: scatter_plane(d).wait_recv(), inner)
         hstage[...] = jnp.sum(gin[...].astype(F32), axis=0).astype(BF16)
         each(lambda d: scatter_line(d).start(), outer)
+        send_terms(batch, 2 * batch)
         hin[z] = hstage[z]
         each(lambda d: scatter_line(d).wait_recv(), outer)
         gall[i, z] = jnp.sum(hin[...].astype(F32), axis=0).astype(BF16)
         each(lambda d: gather_line(d).start(), outer)
+        send_terms(2 * batch, n - 1)
         each(lambda d: gather_line(d).wait_recv(), outer)
         each(lambda d: gather_plane(d).start(), inner)
+    else:
+        send_terms(0, n - 1)
     each(lambda d: term_copy(d).wait(), n)
     if inner:
         each(lambda d: scatter_plane(d).wait_send(), inner)
@@ -396,31 +412,25 @@
         neigh_ref[...] = total[self_ref.shape[0]:]
 
 
-def finish_kernel(hub_dev, edge, send_ref, hub_ref, direct_ref, back_ref, out_ref):
+def finish_kernel(hub_dev, edge, send_ref, hub_ref, direct_hbm, back_ref, out_hbm, total_ref, sem):
     n = back_ref.shape[0]
-    span = out_ref.shape[0]
-    base = pl.program_id(0) * span
-    out_ref[...] = direct_ref[...]
+    load = pltpu.make_async_copy(direct_hbm, total_ref, sem.at[0])
+    load.start()
+    hub_total = jnp.sum(back_ref[:, edge:, :].astype(F32), axis=0)
+    load.wait()
 
     def add(q, carry):
-        place = send_ref[q] * edge - base
-
-        @pl.when((place >= 0) & (place < span))
-        def _():
-            rows = pl.ds(pl.multiple_of(place, edge), edge)
-            out_ref[rows, :] += back_ref[q, 0:edge, :].astype(F32)
-
+        rows = pl.ds(pl.multiple_of(send_ref[q] * edge, edge), edge)
+        total_ref[rows, :] += back_ref[q, 0:edge, :].astype(F32)
         return carry
 
     lax.fori_loop(0, n, add, 0)
     for h in range(hub_dev):
-        place = hub_ref[h] - base
-
-        @pl.when((place >= 0) & (place < span))
-        def _():
-            total = jnp.sum(back_ref[:, edge:, :].astype(F32), axis=0)
-            row = total[h:h + 1] + total[hub_dev + h:hub_dev + h + 1]
-            out_ref[pl.ds(place, 1), :] += row
+        row = hub_total[h:h + 1] + hub_total[hub_dev + h:hub_dev + h + 1]
+        total_ref[pl.ds(hub_ref[h], 1), :] += row
+    store = pltpu.make_async_copy(total_ref, out_hbm, sem.at[1])
+    store.start()
+    store.wait()
 
 
 def shards(
@@ -447,8 +457,8 @@
             sds((n, tall, wide), BF16), sds((tiles, edge, wide), BF16), sds((tiles, edge, wide), BF16),
             sds(self_weight.shape, BF16), sds(neighbor_weight.shape, BF16),
         ),
-        in_specs=[vmem(), anywhere, vmem(), vmem()] + [smem()] * 2,
-        out_specs=(vmem(), anywhere, anywhere, vmem(), vmem()),
+        in_specs=[vmem()] * 4 + [smem()] * 2,
+        out_specs=(vmem(),) * 5,
         scratch_shapes=[
             pltpu.VMEM((n, tall, half), BF16),
             dma((n,)), dma((n,)), dma((n,)), dma((n,)), dma((2,)), dma((4,)), dma((4,)),
@@ -531,14 +541,12 @@
         total = jnp.where(feat_index[0] == 0, total, swapped)
         self_grad, neighbor_grad = total[:half], total[half:]
 
-    steps = math.gcd(tiles, 4)
-    block = pl.BlockSpec((rows // steps, half), lambda i: (i, 0))
     input_grad = pl.pallas_call(
         functools.partial(finish_kernel, hub_dev, edge),
-        grid=(steps,),
         out_shape=sds((rows, half), F32),
-        in_specs=[smem(), smem(), block, pl.BlockSpec((n, tall, half), lambda i: (0, 0, 0))],
-        out_specs=block,
+        in_specs=[smem()] * 2 + [anywhere, vmem()],
+        out_specs=anywhere,
+        scratch_shapes=[pltpu.VMEM((rows, half), F32), dma((2,))],
         compiler_params=params(),
         name="finish",
     )(send_tile, hub_rows, direct.reshape(rows, half), back)

time: 104 us -> 83.9 us (0.81); the launches traced: 104 us -> 82.6 us
  Pallas kernels: 102 us -> 80 us
    pallas_call x1, Pallas kernels: 43.1 us -> 23.9 us  [shards(): pl.pallas_call(functools.partial(exchange_kernel, n, hub_dev), out_shape=...]
    pallas_call x1, Pallas kernels: 33 us -> 30.9 us  [shards(): pl.pallas_call(functools.partial(return_kernel, n, inner, factor), out_sh...]
where the time goes in v5:
time: 83.9 us; the launch traced here: 82.6 us
  Pallas kernels  80 us (95%)
  between operations  1.34 us (2%)
  local copies, waits for them, and re-layouts  1.32 us (2%)
    pallas_call x1, Pallas kernels, shards(): pl.pallas_call(functools.partial(return_kernel, n, inner, factor), out_sh...  30.9 us
    pallas_call x1, Pallas kernels, shards(): pl.pallas_call(functools.partial(exchange_kernel, n, hub_dev), out_shape=...  23.9 us
    pallas_call x1, Pallas kernels, shards(): pl.pallas_call(functools.partial(local_kernel, hub_dev), out_shape=(sds((...  21 us
    pallas_call x1, Pallas kernels, shards(): pl.pallas_call(functools.partial(finish_kernel, hub_dev, edge), out_shape...  4.21 us

profile of v5, /device:TPU:0, one launch (start us, length us, event | category | flops | bytes accessed | tf_op | source)
XLA Modules:
  0.0 82.6 jit_solution(10021861344834841841)
XLA Ops:
  1.3 23.9 %exchange.1 = (bf16[16,144,256]{2,1,0:T(8,128)(2,1)}, bf16[32,128,256]{2,1,0:T(8,128)(2,1)}, bf16[32,128,256]{2,1,0:T(8,128)(2,1)}, bf16[128,256]{1,0:T(8,128)(2,1)}, bf16[128,256]{1,0:T(8,128)(2,1)}) custom-call(bf16[32,128,128]{2,1,0:T(8,128)(2,1)} %bitcast.7, bf16[32,128,128]{2,1,0:T(8,128)(2,1)} %bitcast.8, bf16[128,256]{1,0:T(8,128)(2,1)} %ws_ref.3, ...), custom_call_target="tpu_custom_call" | custom-call | tf_op jit(solution)/shard_map/exchange/pallas_call | solution.py:454
  25.2 21.0 %local_pass.1 = (bf16[32,128,128]{2,1,0:T(8,128)(2,1)}, f32[256,256]{1,0:T(8,128)}, f32[32,128,128]{2,1,0:T(8,128)}, bf16[16,144,128]{2,1,0:T(8,128)(2,1)}) custom-call(s32[1]{0:T(128)} %bitcast.feat_ref, s32[160]{0:T(256)} %row_ref.1, s32[160]{0:T(256)} %owner_ref.1, s32[1]{0:T(128)S(6)} %copy.17.count_ref, ...), custom_call_target="tpu_custom_call" | custom-call | tf_op jit(solution)/shard_map/local_pass/pallas_call | solution.py:477
  46.2 30.9 %send_back.1 = (bf16[16,144,128]{2,1,0:T(8,128)(2,1)}, f32[128,256]{1,0:T(8,128)}, f32[128,256]{1,0:T(8,128)}) custom-call(bf16[16,144,128]{2,1,0:T(8,128)(2,1)} %get-tuple-element.22.refs_0_, f32[256,256]{1,0:T(8,128)} %get-tuple-element.23.refs_1_), custom_call_target="tpu_custom_call" | custom-call | tf_op jit(solution)/shard_map/send_back/pallas_call | solution.py:514
  77.1 0.0 copy-start.1
  77.1 0.0 copy-start
  77.1 4.2 %finish.1 = f32[4096,128]{1,0:T(8,128)} custom-call(s32[16]{0:T(128)} %send_ref.3, s32[2]{0:T(128)} %hub_ref.3, f32[4096,128]{1,0:T(8,128)} %bitcast.6, bf16[16,144,128]{2,1,0:T(8,128)(2,1)} %get-tuple-element.27.back_ref), custom_call_target="tpu_custom_call" | custom-call | tf_op jit(solution)/shard_map/finish/pallas_call | solution.py:544
  81.3 0.0 copy-done.1
  81.3 0.7 copy.18
  82.0 0.0 copy-done
  82.0 0.7 copy.19
Async XLA Ops:
  77.1 4.2 %copy-start.1 = (f32[128,256]{1,0:T(8,128)S(1)}, f32[128,256]{1,0:T(8,128)}, u32[]{:S(2)}) copy-start(f32[128,256]{1,0:T(8,128)} %get-tuple-element.33) | copy-start | bytes 393220
  77.1 4.9 %copy-start = (f32[128,256]{1,0:T(8,128)S(1)}, f32[128,256]{1,0:T(8,128)}, u32[]{:S(2)}) copy-start(f32[128,256]{1,0:T(8,128)} %get-tuple-element.34) | copy-start | bytes 393220

commit v6 on v5

--- a/solution.py
+++ b/solution.py
@@ -50,7 +50,7 @@
 
 def exchange_kernel(
     n, hub_dev, feat_ref, cot_ref, ws_ref, wn_ref, send_ref, hub_ref,
-    cols_ref, x_ref, c_ref, wso_ref, wno_ref,
+    cols_ref, x_ref, c_ref, wso_ref, wno_ref, xt_ref,
     stage, send_sem, recv_sem, fsend_sem, frecv_sem, loc_sem, esend_sem, erecv_sem,
 ):
     me = lax.axis_index("dom")
@@ -60,6 +60,7 @@
     pad = stage.shape[1] - edge
     half = feat_ref.shape[2]
     greet(n, me, feat, True)
+    wait_greetings(n)
 
     row_ids = lax.broadcasted_iota(jnp.int32, (edge, half), 0)
     out_ids = lax.broadcasted_iota(jnp.int32, (pad, half), 0)
@@ -71,16 +72,6 @@
         hub_block = jnp.where(out_ids == h, row, hub_block)
     hub_block = hub_block.astype(BF16)
 
-    def fill(d, carry):
-        stage[d, 0:edge, :] = feat_ref[send_ref[lax.rem(me + d, n)]]
-        stage[d, edge:, :] = hub_block
-        return carry
-
-    lax.fori_loop(1, n, fill, 0)
-    cols_ref[me, 0:edge, 0:half] = feat_ref[send_ref[me]]
-    cols_ref[me, edge:, 0:half] = hub_block
-    wait_greetings(n)
-
     def peer_copy(d):
         return pltpu.make_async_remote_copy(
             src_ref=stage.at[d], dst_ref=cols_ref.at[me, :, 0:half],
@@ -95,11 +86,16 @@
             device_id={"feat": 1 - feat}, device_id_type=pl.DeviceIdType.MESH,
         )
 
-    def send(k, carry):
-        peer_copy(mixed(k, n)).start()
-        return carry
-
-    lax.fori_loop(0, n - 1, send, 0)
+    def send(d, carry):
+        q = lax.rem(me + d, n)
+        stage[d, 0:edge, :] = feat_ref[send_ref[q]]
+        stage[d, edge:, :] = hub_block
+        peer_copy(d).start()
+        return carry
+
+    lax.fori_loop(1, n, send, 0)
+    cols_ref[me, 0:edge, 0:half] = feat_ref[send_ref[me]]
+    cols_ref[me, edge:, 0:half] = hub_block
     forward(me).start()
 
     extras = [
@@ -123,13 +119,15 @@
     for copy in locals_:
         copy.start()
 
-    def arrive(k, carry):
-        d = mixed(k, n)
+    for t in range(feat_ref.shape[0]):
+        xt_ref[:, t * edge:(t + 1) * edge] = feat_ref[t].T
+
+    def arrive(d, carry):
         peer_copy(d).wait_recv()
         forward(lax.rem(me - d + n, n)).start()
         return carry
 
-    lax.fori_loop(0, n - 1, arrive, 0)
+    lax.fori_loop(1, n, arrive, 0)
     for copy in locals_:
         copy.wait()
     for copy in extras:
@@ -167,9 +165,9 @@
 
 def local_kernel(
     hub_dev, feat_ref, row_ref, owner_ref, count_ref,
-    cols_ref, x_hbm, c_hbm, ws_ref, wn_ref, wso_ref, wno_ref, val_hbm, panel_ref,
+    cols_ref, x_hbm, c_hbm, ws_ref, wn_ref, wso_ref, wno_ref, val_hbm, panel_ref, xt_hbm,
     out_hbm, grad_ref, direct_hbm, terms_ref,
-    acc, sq, slopes_t, terms_t, hub_s, x_ref, c_ref, val_ref, out_ref, direct_ref, w_ahead, w_back,
+    acc, sq, slopes_t, terms_t, hub_s, x_ref, c_ref, xt_ref, val_ref, out_ref, direct_ref, w_ahead, w_back,
     val_sem, in_sem, out_sem, direct_sem,
 ):
     f = feat_ref[0]
@@ -200,8 +198,10 @@
         val_copy(i).start()
     x_copy = pltpu.make_async_copy(x_hbm, x_ref, in_sem.at[0])
     c_copy = pltpu.make_async_copy(c_hbm, c_ref, in_sem.at[1])
+    xt_copy = pltpu.make_async_copy(xt_hbm, xt_ref, in_sem.at[2])
     x_copy.start()
     c_copy.start()
+    xt_copy.start()
 
     def local_order(w):
         return jnp.where(f == 0, w, jnp.concatenate([w[:, half:], w[:, :half]], axis=1))
@@ -256,6 +256,7 @@
     ones = jnp.ones((2 * edge, half), BF16)
     x_copy.wait()
     c_copy.wait()
+    xt_copy.wait()
 
     def dense(i, carry):
         span = pl.ds(i * group, group)
@@ -279,8 +280,9 @@
         back_t = back.T
         for g in range(group):
             slopes_t[i * group + g] = back_t[:, g * edge:(g + 1) * edge]
-        left = jnp.concatenate([x[:, :half], aggregate[:, :half]], axis=1)
-        grad_ref[...] += dot(left, slopes, ((0,), (0,)))
+        x_turned = xt_ref[:, pl.ds(pl.multiple_of(i * rows, rows), rows)]
+        grad_ref[0:half] += dot(x_turned, slopes)
+        grad_ref[half:] += dot(aggregate[:, :half], slopes, ((0,), (0,)))
         return carry
 
     lax.fori_loop(0, tiles // group, dense, 0)
@@ -308,7 +310,7 @@
     terms_ref[:, edge:, :] = blocks.reshape(n, pad, half).astype(BF16)
 
     def emit(o, carry):
-        terms_ref[o, 0:edge, :] = terms_t[o].T.astype(BF16)
+        terms_ref[o, 0:edge, :] = terms_t[o].astype(BF16).T
         return carry
 
     lax.fori_loop(0, n, emit, 0)
@@ -321,10 +323,10 @@
     lax.fori_loop(0, tiles // group, drain, 0)
 
 
-def return_kernel(n, inner, factor, *refs):
+def return_kernel(n, inner, *refs):
     if inner:
-        (terms_ref, grad_ref, back_ref, self_ref, neigh_ref,
-         send_sem, recv_sem, gstage, gin, hstage, hin, gall, step_send, step_recv) = refs
+        (terms_ref, grad_ref, back_ref, gall,
+         send_sem, recv_sem, gstage, gin, hstage, hin, step_send, step_recv) = refs
     else:
         terms_ref, back_ref, send_sem, recv_sem = refs
     me = lax.axis_index("dom")
@@ -405,32 +407,31 @@
         each(lambda d: scatter_line(d).wait_send(), outer)
         each(lambda d: gather_line(d).wait_send(), outer)
         each(lambda d: gather_plane(d).wait(), inner)
-        total = gall[...].astype(F32).reshape(grad_ref.shape) * factor
-        half = total.shape[1] // 2
-        total = jnp.where(feat == 0, total, jnp.concatenate([total[:, half:], total[:, :half]], axis=1))
-        self_ref[...] = total[: self_ref.shape[0]]
-        neigh_ref[...] = total[self_ref.shape[0]:]
-
-
-def finish_kernel(hub_dev, edge, send_ref, hub_ref, direct_hbm, back_ref, out_hbm, total_ref, sem):
+
+
+def finish_kernel(
+    hub_dev, edge, factor, send_ref, hub_ref, feat_ref, direct_ref, back_ref, sum_ref,
+    out_ref, self_ref, neigh_ref,
+):
     n = back_ref.shape[0]
-    load = pltpu.make_async_copy(direct_hbm, total_ref, sem.at[0])
-    load.start()
-    hub_total = jnp.sum(back_ref[:, edge:, :].astype(F32), axis=0)
-    load.wait()
+    half = out_ref.shape[1]
+    out_ref[...] = direct_ref[...]
 
     def add(q, carry):
         rows = pl.ds(pl.multiple_of(send_ref[q] * edge, edge), edge)
-        total_ref[rows, :] += back_ref[q, 0:edge, :].astype(F32)
+        out_ref[rows, :] += back_ref[q, 0:edge, :].astype(F32)
         return carry
 
     lax.fori_loop(0, n, add, 0)
+    hub_total = jnp.sum(back_ref[:, edge:, :].astype(F32), axis=0)
     for h in range(hub_dev):
         row = hub_total[h:h + 1] + hub_total[hub_dev + h:hub_dev + h + 1]
-        total_ref[pl.ds(hub_ref[h], 1), :] += row
-    store = pltpu.make_async_copy(total_ref, out_hbm, sem.at[1])
-    store.start()
-    store.wait()
+        out_ref[pl.ds(hub_ref[h], 1), :] += row
+    total = sum_ref[...].astype(F32) * factor
+    swapped = jnp.concatenate([total[:, half:], total[:, :half]], axis=1)
+    total = jnp.where(feat_ref[0] == 0, total, swapped)
+    self_ref[...] = total[:half]
+    neigh_ref[...] = total[half:]
 
 
 def shards(
@@ -451,14 +452,14 @@
     anywhere = pl.BlockSpec(memory_space=pl.ANY)
     params = functools.partial(pltpu.CompilerParams, vmem_limit_bytes=VMEM_BYTES)
 
-    cols, x_all, c_all, ws_other, wn_other = pl.pallas_call(
+    cols, x_all, c_all, ws_other, wn_other, x_turned = pl.pallas_call(
         functools.partial(exchange_kernel, n, hub_dev),
         out_shape=(
             sds((n, tall, wide), BF16), sds((tiles, edge, wide), BF16), sds((tiles, edge, wide), BF16),
-            sds(self_weight.shape, BF16), sds(neighbor_weight.shape, BF16),
+            sds(self_weight.shape, BF16), sds(neighbor_weight.shape, BF16), sds((half, rows), BF16),
         ),
         in_specs=[vmem()] * 4 + [smem()] * 2,
-        out_specs=(vmem(),) * 5,
+        out_specs=(vmem(),) * 6,
         scratch_shapes=[
             pltpu.VMEM((n, tall, half), BF16),
             dma((n,)), dma((n,)), dma((n,)), dma((n,)), dma((2,)), dma((4,)), dma((4,)),
@@ -480,7 +481,7 @@
             sds((tiles, edge, half), BF16), sds((wide, wide), F32),
             sds((tiles, edge, half), F32), sds((n, tall, half), BF16),
         ),
-        in_specs=[smem()] * 4 + [vmem(), anywhere, anywhere] + [vmem()] * 4 + [anywhere, vmem()],
+        in_specs=[smem()] * 4 + [vmem(), anywhere, anywhere] + [vmem()] * 4 + [anywhere, vmem(), anywhere],
         out_specs=(anywhere, vmem(), anywhere, vmem()),
         scratch_shapes=[
             pltpu.VMEM((tiles, edge, wide), F32),
@@ -490,18 +491,20 @@
             pltpu.VMEM((hubs, half), F32),
             pltpu.VMEM((tiles, edge, wide), BF16),
             pltpu.VMEM((tiles, edge, wide), BF16),
+            pltpu.VMEM((half, rows), BF16),
             pltpu.VMEM(tile_values.shape, BF16),
             pltpu.VMEM((tiles, edge, half), BF16),
             pltpu.VMEM((tiles, edge, half), F32),
             pltpu.VMEM((2 * wide, wide), BF16),
             pltpu.VMEM((wide, wide), BF16),
-            dma((parts,)), dma((2,)), dma((chunks,)), dma((chunks,)),
+            dma((parts,)), dma((3,)), dma((chunks,)), dma((chunks,)),
         ],
         compiler_params=params(),
         name="local_pass",
     )(
         feat_index, tile_row, tile_owner, tile_count, cols, x_all, c_all,
         self_weight, neighbor_weight, ws_other, wn_other, tile_values, hub_panel.T,
+        x_turned,
     )
 
     factor = 1.0 / math.sqrt(rows * n)
@@ -511,16 +514,15 @@
     back_shape = sds((n, tall, half), BF16)
     if inner:
         line = (inner, wide // n, wide)
-        back, self_grad, neighbor_grad = pl.pallas_call(
-            functools.partial(return_kernel, n, inner, factor),
-            out_shape=(back_shape, sds((half, wide), F32), sds((half, wide), F32)),
+        back, sums = pl.pallas_call(
+            functools.partial(return_kernel, n, inner),
+            out_shape=(back_shape, sds((inner,) + line, BF16)),
             in_specs=[vmem()] * 2,
-            out_specs=(vmem(),) * 3,
+            out_specs=(vmem(),) * 2,
             scratch_shapes=[
                 dma((n,)), dma((n,)),
                 pltpu.VMEM((inner,) + line, BF16), pltpu.VMEM((inner,) + line, BF16),
                 pltpu.VMEM(line, BF16), pltpu.VMEM(line, BF16),
-                pltpu.VMEM((inner,) + line, BF16),
                 dma((4, inner)), dma((4, inner)),
             ],
             compiler_params=params(collective_id=1, has_side_effects=True),
@@ -528,7 +530,7 @@
         )(terms, grads)
     else:
         back = pl.pallas_call(
-            functools.partial(return_kernel, n, 0, factor),
+            functools.partial(return_kernel, n, 0),
             out_shape=back_shape,
             in_specs=[vmem()],
             out_specs=vmem(),
@@ -536,20 +538,16 @@
             compiler_params=params(collective_id=1, has_side_effects=True),
             name="send_back",
         )(terms)
-        total = lax.psum(grads, "dom") * factor
-        swapped = jnp.concatenate([total[:, half:], total[:, :half]], axis=1)
-        total = jnp.where(feat_index[0] == 0, total, swapped)
-        self_grad, neighbor_grad = total[:half], total[half:]
-
-    input_grad = pl.pallas_call(
-        functools.partial(finish_kernel, hub_dev, edge),
-        out_shape=sds((rows, half), F32),
-        in_specs=[smem()] * 2 + [anywhere, vmem()],
-        out_specs=anywhere,
-        scratch_shapes=[pltpu.VMEM((rows, half), F32), dma((2,))],
+        sums = lax.psum(grads, "dom")
+
+    input_grad, self_grad, neighbor_grad = pl.pallas_call(
+        functools.partial(finish_kernel, hub_dev, edge, factor),
+        out_shape=(sds((rows, half), F32), sds((half, wide), F32), sds((half, wide), F32)),
+        in_specs=[smem()] * 3 + [vmem()] * 3,
+        out_specs=(vmem(),) * 3,
         compiler_params=params(),
         name="finish",
-    )(send_tile, hub_rows, direct.reshape(rows, half), back)
+    )(send_tile, hub_rows, feat_index, direct.reshape(rows, half), back, sums.reshape(wide, wide))
     return layer.reshape(rows, half), self_grad, neighbor_grad, input_grad
 
 

time: 83.9 us -> 79.4 us (0.946)
  Pallas kernels: 80 us -> 77.6 us
  local copies, waits for them, and re-layouts: 1.32 us -> 0 us
    pallas_call x1, Pallas kernels: 21 us -> 17.6 us  [shards(): pl.pallas_call(functools.partial(local_kernel, hub_dev), out_shape=(sds((...]
    pallas_call x2, Pallas kernels: 35.1 us -> 37.8 us  [the longest x1 34.3 us: shards(): pl.pallas_call(functools.partial(return_kernel, n, inner), out_shape=(bac...]
    pallas_call x1, Pallas kernels: 23.9 us -> 22.2 us  [shards(): pl.pallas_call(functools.partial(exchange_kernel, n, hub_dev), out_shape=...]
    unnamed x6 -> x0, local copies, waits for them, and re-layouts: 1.32 us -> none
where the time goes in v6:
time: 79.4 us; the launch traced here: 78.9 us
  Pallas kernels  77.6 us (98%)
  between operations  1.3 us (2%)
    pallas_call x1, Pallas kernels, shards(): pl.pallas_call(functools.partial(return_kernel, n, inner), out_shape=(bac...  34.3 us
    pallas_call x1, Pallas kernels, shards(): pl.pallas_call(functools.partial(exchange_kernel, n, hub_dev), out_shape=...  22.2 us
    pallas_call x1, Pallas kernels, shards(): pl.pallas_call(functools.partial(local_kernel, hub_dev), out_shape=(sds((...  17.6 us
    pallas_call x1, Pallas kernels, shards(): pl.pallas_call(functools.partial(finish_kernel, hub_dev, edge, factor), o...  3.53 us

profile of v6, /device:TPU:0, one launch (start us, length us, event | category | flops | bytes accessed | tf_op | source)
XLA Modules:
  0.0 78.9 jit_solution(10452035172845993305)
XLA Ops:
  1.3 22.2 %exchange.1 = (bf16[16,144,256]{2,1,0:T(8,128)(2,1)}, bf16[32,128,256]{2,1,0:T(8,128)(2,1)}, bf16[32,128,256]{2,1,0:T(8,128)(2,1)}, bf16[128,256]{1,0:T(8,128)(2...) custom-call(bf16[32,128,128]{2,1,0:T(8,128)(2,1)} %bitcast.8, bf16[32,128,128]{2,1,0:T(8,128)(2,1)} %bitcast.9, ...), custom_call_target="tpu_custom_call" | custom-call | tf_op jit(solution)/shard_map/exchange/pallas_call | solution.py:455
  23.5 17.6 %local_pass.1 = (bf16[32,128,128]{2,1,0:T(8,128)(2,1)}, f32[256,256]{1,0:T(8,128)}, f32[32,128,128]{2,1,0:T(8,128)}, bf16[16,144,128]{2,1,0:T(8,128)(2,1)}) custom-call(s32[1]{0:T(128)} %bitcast.feat_ref, s32[160]{0:T(256)} %row_ref.1, s32[160]{0:T(256)} %owner_ref.1, s32[1]{0:T(128)S(6)} %copy.15.count_ref, ...), custom_call_target="tpu_custom_call" | custom-call | tf_op jit(solution)/shard_map/local_pass/pallas_call | solution.py:478
  41.1 34.3 %send_back.1 = (bf16[16,144,128]{2,1,0:T(8,128)(2,1)}, bf16[4,4,16,256]{3,2,1,0:T(8,128)(2,1)}) custom-call(bf16[16,144,128]{2,1,0:T(8,128)(2,1)} %get-tuple-element.27.refs_0_, f32[256,256]{1,0:T(8,128)} %get-tuple-element.28.refs_1_), custom_call_target="tpu_custom_call" | custom-call | tf_op jit(solution)/shard_map/send_back/pallas_call | solution.py:517
  75.4 3.5 %finish.1 = (f32[4096,128]{1,0:T(8,128)}, f32[128,256]{1,0:T(8,128)}, f32[128,256]{1,0:T(8,128)}) custom-call(s32[16]{0:T(128)} %send_ref.3, s32[2]{0:T(128)} %hub_ref.3, s32[1]{0:T(128)} %bitcast.feat_ref, f32[4096,128]{1,0:T(8,128)} %bitcast.7, bf16[16,144,128]{2,1,0:T(8,128)(2,1)} %get-tuple-element.29.back_ref, bf16[256,256]{1,0:T(8,128)(2,1)} %bitcast.11), custom_call_target="tpu_custom_call" | custom-call | tf_op jit(solution)/shard_map/finish/pallas_call | solution.py:543

commit v7 on v6

--- a/solution.py
+++ b/solution.py
@@ -11,7 +11,7 @@
 F32 = jnp.float32
 BF16 = jnp.bfloat16
 VMEM_BYTES = 58 * 2**20
-UNROLL = 8
+UNROLL = 10
 
 
 def vmem():
@@ -473,7 +473,7 @@
 
     feat_index = lax.axis_index("feat").astype(jnp.int32).reshape(1)
     slots = tile_values.shape[0]
-    parts = math.gcd(slots, 8)
+    parts = math.gcd(slots, 4)
     chunks = tiles // math.gcd(tiles, 4)
     layer, grads, direct, terms = pl.pallas_call(
         functools.partial(local_kernel, hub_dev),

time: 79.4 us -> 77 us (0.970)
  Pallas kernels: 77.6 us -> 74.4 us
    pallas_call x1, Pallas kernels: 34.3 us -> 32.4 us  [shards(): pl.pallas_call(functools.partial(return_kernel, n, inner), out_shape=(bac...]
    pallas_call x1, Pallas kernels: 17.6 us -> 16.3 us  [shards(): pl.pallas_call(functools.partial(local_kernel, hub_dev), out_shape=(sds((...]
where the time goes in v7:
time: 77 us; the launch traced here: 75.7 us
  Pallas kernels  74.4 us (97%)
  between operations  1.3 us (2%)
    pallas_call x1, Pallas kernels, shards(): pl.pallas_call(functools.partial(return_kernel, n, inner), out_shape=(bac...  32.4 us
    pallas_call x1, Pallas kernels, shards(): pl.pallas_call(functools.partial(exchange_kernel, n, hub_dev), out_shape=...  22.2 us
    pallas_call x1, Pallas kernels, shards(): pl.pallas_call(functools.partial(local_kernel, hub_dev), out_shape=(sds((...  16.3 us
    pallas_call x1, Pallas kernels, shards(): pl.pallas_call(functools.partial(finish_kernel, hub_dev, edge, factor), o...  3.53 us

profile of v7, /device:TPU:0, one launch (start us, length us, event | category | flops | bytes accessed | tf_op | source)
XLA Modules:
  0.0 75.7 jit_solution(1441844789257041475)
XLA Ops:
  1.3 22.2 %exchange.1 = (bf16[16,144,256]{2,1,0:T(8,128)(2,1)}, bf16[32,128,256]{2,1,0:T(8,128)(2,1)}, bf16[32,128,256]{2,1,0:T(8,128)(2,1)}, bf16[128,256]{1,0:T(8,128)(2...) custom-call(bf16[32,128,128]{2,1,0:T(8,128)(2,1)} %bitcast.8, bf16[32,128,128]{2,1,0:T(8,128)(2,1)} %bitcast.9, ...), custom_call_target="tpu_custom_call" | custom-call | tf_op jit(solution)/shard_map/exchange/pallas_call | solution.py:455
  23.5 16.3 %local_pass.1 = (bf16[32,128,128]{2,1,0:T(8,128)(2,1)}, f32[256,256]{1,0:T(8,128)}, f32[32,128,128]{2,1,0:T(8,128)}, bf16[16,144,128]{2,1,0:T(8,128)(2,1)}) custom-call(s32[1]{0:T(128)} %bitcast.feat_ref, s32[160]{0:T(256)} %row_ref.1, s32[160]{0:T(256)} %owner_ref.1, s32[1]{0:T(128)S(6)} %copy.15.count_ref, ...), custom_call_target="tpu_custom_call" | custom-call | tf_op jit(solution)/shard_map/local_pass/pallas_call | solution.py:478
  39.8 32.4 %send_back.1 = (bf16[16,144,128]{2,1,0:T(8,128)(2,1)}, bf16[4,4,16,256]{3,2,1,0:T(8,128)(2,1)}) custom-call(bf16[16,144,128]{2,1,0:T(8,128)(2,1)} %get-tuple-element.27.refs_0_, f32[256,256]{1,0:T(8,128)} %get-tuple-element.28.refs_1_), custom_call_target="tpu_custom_call" | custom-call | tf_op jit(solution)/shard_map/send_back/pallas_call | solution.py:517
  72.2 3.5 %finish.1 = (f32[4096,128]{1,0:T(8,128)}, f32[128,256]{1,0:T(8,128)}, f32[128,256]{1,0:T(8,128)}) custom-call(s32[16]{0:T(128)} %send_ref.3, s32[2]{0:T(128)} %hub_ref.3, s32[1]{0:T(128)} %bitcast.feat_ref, f32[4096,128]{1,0:T(8,128)} %bitcast.7, bf16[16,144,128]{2,1,0:T(8,128)(2,1)} %get-tuple-element.29.back_ref, bf16[256,256]{1,0:T(8,128)(2,1)} %bitcast.11), custom_call_target="tpu_custom_call" | custom-call | tf_op jit(solution)/shard_map/finish/pallas_call | solution.py:543
